TPU v7x, 32 devices: a whole 2x2x4 slice. The times are simulated.
32 devices in a mesh: dp: 16 (over z, x, core), mp: 2 (over y).
Axes of the slice: x: 2, y: 2, z: 4, core: 2. Of those that a mesh axis runs over, the one named last changes fastest.
Arguments:
- hidden_in: bfloat16 [32768, 1024], P(('dp', 'mp')), may hold values from -6 to 6
- query_weight: bfloat16 [1024, 1024], replicated, may hold values from -0.1875 to 0.1875
- key_weight: bfloat16 [1024, 1024], replicated, may hold values from -0.1875 to 0.1875
- value_weight: bfloat16 [1024, 1024], replicated, may hold values from -0.1875 to 0.1875
- select_weight: bfloat16 [1024, 1024], replicated, may hold values from -0.1875 to 0.1875
- out_weight: bfloat16 [1024, 1024], replicated, may hold values from -0.1875 to 0.1875
- first_weight: bfloat16 [1024, 2816], P(None, 'mp'), may hold values from -0.1875 to 0.1875
- second_weight: bfloat16 [1024, 2816], P(None, 'mp'), may hold values from -0.1875 to 0.1875
- down_weight: bfloat16 [2816, 1024], P('mp'), may hold values from -0.109375 to 0.109375
- decay_slope: float32 [8], replicated, may hold values from 0.00012207031 to 0.5
- doc_lengths: int32 [16, 3], P('dp'), may hold values from 384 to 1024, as said below
- cotangent: bfloat16 [32768, 1024], P(('dp', 'mp')), may hold values from -6 to 6
Outputs:
- output: bfloat16 [32768, 1024], P(('dp', 'mp'))
- grad_hidden: bfloat16 [32768, 1024], P(('dp', 'mp'))
- grad_query: float32 [1024, 1024], P('dp', 'mp')
- grad_key: float32 [1024, 1024], P('dp', 'mp')
- grad_value: float32 [1024, 1024], P('dp', 'mp')
- grad_select: float32 [1024, 1024], P('dp', 'mp')
- grad_out: float32 [1024, 1024], P('dp', 'mp')
- grad_first: float32 [1024, 2816], P('dp', 'mp')
- grad_second: float32 [1024, 2816], P('dp', 'mp')
- grad_down: float32 [2816, 1024], P('mp', 'dp')
Inputs may be any that keep to these rules, and one draw needn't show every extreme that they name: `doc_lengths`: row g gives the lengths of the 3 documents packed in order from the first of the group's 2048 rows; the rows after them are padding. Two of the documents have 2048 // 4 tokens and one has 1024, which one is drawn; the last document gives up 0 to 128 of its tokens to padding.
All inputs are finite; a program needn't handle non-finite values.
Results may differ from a plain program's by a relative error of at most 0.019.
Values may be sent and summed in bfloat16 or wider, within the bound.
A program may use at most 320 MiB of HBM per device.

v0:
```python
import jax
import jax.numpy as jnp
from jax import lax
from jax.sharding import PartitionSpec as P

HEAD = 128


EPSILON = 1e-06
HIGHEST = lax.Precision.HIGHEST


def entering(shard, axis, combine, identity):
    peers, index = (lax.axis_size(axis), lax.axis_index(axis))
    everything = jax.tree.map(
        lambda part, kind: lax.all_gather(part.astype(kind), axis),
        shard,
        (jnp.bfloat16, jnp.bfloat16),
    )
    start = jax.tree.map(
        lambda part, zero: jnp.broadcast_to(jnp.asarray(zero, part.dtype), part.shape),
        shard,
        identity,
    )

    def step(k, before):
        reached = k < index
        new = combine(
            before, jax.tree.map(lambda part, own: part[k].astype(own.dtype), everything, shard)
        )
        return jax.tree.map(lambda a, b: jnp.where(reached, a, b), new, before)

    return lax.fori_loop(0, peers, step, start)


def carried_in(shard, axis, join, neutral):
    count = lax.axis_size(axis)
    place = lax.axis_index(axis)
    ahead = count - 1 - place
    gathered = jax.tree.map(
        lambda a, kind: lax.all_gather(a.astype(kind), axis),
        shard,
        jax.tree.map(lambda a: jnp.bfloat16 if a.dtype == jnp.float32 else a.dtype, shard),
    )
    state = jax.tree.map(lambda a, e: jnp.zeros_like(a) + jnp.asarray(e, a.dtype), shard, neutral)

    def one(step, state):
        source = count - 1 - step
        return join(
            state,
            jax.tree.map(
                lambda a, own: lax.dynamic_index_in_dim(a, source, 0, False).astype(own.dtype),
                gathered,
                shard,
            ),
        )

    return lax.fori_loop(0, ahead, one, state)


def matmul(left, right):
    return jnp.dot(left, right, preferred_element_type=jnp.float32)


def contract_rows(left, right):
    return lax.dot_general(
        left, right, (((0,), (0,)), ((), ())), preferred_element_type=jnp.float32
    )


def contract_cols(left, right):
    return lax.dot_general(
        left, right, (((1,), (1,)), ((), ())), preferred_element_type=jnp.float32
    )


def scale_of(values):
    return lax.rsqrt(jnp.mean(values * values, axis=-1, keepdims=True) + EPSILON)


def norm_back(values, scale, upstream):
    return scale * upstream - values * (scale * scale * scale) * jnp.mean(
        values * upstream, axis=-1, keepdims=True
    )


def rotate(values, position):
    freq = 10000.0 ** (-jnp.arange(HEAD, dtype=jnp.float32) / HEAD)
    phase = position.astype(jnp.float32)[:, None] * freq[None, :]
    return jnp.concatenate(
        [values * jnp.cos(phase)[:, None, :], values * jnp.sin(phase)[:, None, :]], axis=-1
    )


def local_layout(lengths, offset, count):
    ends = jnp.cumsum(lengths)
    starts = ends - lengths
    places = offset + jnp.arange(count, dtype=jnp.int32)
    segment = jnp.sum((places[:, None] >= ends[None, :]).astype(jnp.int32), axis=1)
    numbers = jnp.arange(lengths.shape[0], dtype=jnp.int32)
    begin = jnp.sum(jnp.where(segment[:, None] == numbers[None, :], starts[None, :], 0), axis=1)
    position = jnp.where(segment < lengths.shape[0], places - begin, 0)
    before = offset - 1
    prior = jnp.where(before >= 0, jnp.sum((before >= ends).astype(jnp.int32)), -1)
    return (segment, position, prior)


def combine(earlier, later):
    return (earlier[0] * later[0], later[0][:, None, None] * earlier[1] + later[1])


def per_device(
    hidden_in,
    query_weight,
    key_weight,
    value_weight,
    select_weight,
    out_weight,
    first_weight,
    second_weight,
    down_weight,
    decay_slope,
    doc_lengths,
    cotangent,
):
    count = hidden_in.shape[0]
    width = hidden_in.shape[1]
    heads = width // HEAD
    docs = doc_lengths.shape[1]
    offset = lax.axis_index("mp") * count
    segment, position, prior = local_layout(doc_lengths[0], offset, count)
    live = segment < docs
    step_index = jnp.arange(count, dtype=jnp.int32)
    gap = (step_index[:, None] - step_index[None, :]).astype(jnp.float32)
    allowed = (gap >= 0) & (segment[:, None] == segment[None, :]) & live[:, None]
    decay_table = jnp.where(
        allowed[None], jnp.exp(-decay_slope[:, None, None] * jnp.maximum(gap, 0.0)[None]), 0.0
    )
    final = segment[count - 1]
    fade_out = (
        jnp.exp(-decay_slope[None, :] * (count - 1 - step_index)[:, None].astype(jnp.float32))
        * ((segment == final) & live).astype(jnp.float32)[:, None]
    )
    fade_in = (
        jnp.exp(-decay_slope[None, :] * (step_index[:, None] + 1).astype(jnp.float32))
        * ((segment == prior) & live).astype(jnp.float32)[:, None]
    )
    carry_factor = ((final == prior) & (final < docs)).astype(jnp.float32) * jnp.exp(
        -decay_slope * count
    )

    def local_part(queries, keys, value_heads):
        scores = jnp.einsum("thd,shd->hts", queries, keys, precision=HIGHEST) * decay_table
        result = jnp.einsum("hts,she->the", scores, value_heads, precision=HIGHEST)
        state = jnp.einsum(
            "shd,she->hde", keys * fade_out[:, :, None], value_heads, precision=HIGHEST
        )
        return (result, state)

    def carried_part(queries, incoming):
        return fade_in[:, :, None] * jnp.einsum(
            "thd,hde->the", queries, incoming, precision=HIGHEST
        )

    def features(query_pre, key_pre):
        return (
            rotate(jax.nn.silu(query_pre).reshape(count, heads, HEAD), position),
            rotate(jax.nn.silu(key_pre).reshape(count, heads, HEAD), position),
        )

    hidden = hidden_in.astype(jnp.float32)
    scale_one = scale_of(hidden)
    normed = (hidden * scale_one).astype(jnp.bfloat16)
    query_pre = matmul(normed, query_weight)
    key_pre = matmul(normed, key_weight)
    values = matmul(normed, value_weight)
    select = matmul(normed, select_weight)
    (queries, keys), feature_back = jax.vjp(features, query_pre, key_pre)
    value_heads = values.reshape(count, heads, HEAD)
    (inside, local_state), local_back = jax.vjp(local_part, queries, keys, value_heads)
    identity = (jnp.ones_like(carry_factor), jnp.zeros_like(local_state))
    carried_total = entering((carry_factor, local_state), "mp", combine, identity)
    carried, carried_back = jax.vjp(carried_part, queries, carried_total[1])
    attended = (inside + carried).reshape(count, width)
    scale_two = scale_of(attended)
    normal_att = attended * scale_two
    mixed = (normal_att * select).astype(jnp.bfloat16)
    middle = hidden + matmul(mixed, out_weight)
    scale_three = scale_of(middle)
    second_in = (middle * scale_three).astype(jnp.bfloat16)
    gathered = lax.all_gather(second_in, "mp", axis=0, tiled=True)
    left_part = matmul(gathered, first_weight)
    right_part = matmul(gathered, second_weight)
    inner = (left_part * right_part).astype(jnp.bfloat16)
    branch_sum = lax.psum_scatter(
        matmul(inner, down_weight).astype(jnp.bfloat16), "mp", scatter_dimension=0, tiled=True
    ).astype(jnp.float32)
    output = (middle + branch_sum).astype(jnp.bfloat16)
    cotangent_all = lax.all_gather(cotangent, "mp", axis=0, tiled=True)
    grad_inner = contract_cols(cotangent_all, down_weight)
    grad_left = (grad_inner * right_part).astype(jnp.bfloat16)
    grad_right = (grad_inner * left_part).astype(jnp.bfloat16)
    down_local = contract_rows(cotangent_all, inner)
    first_local = contract_rows(gathered, grad_left)
    second_local = contract_rows(gathered, grad_right)
    grad_second_in = lax.psum_scatter(
        (contract_cols(grad_left, first_weight) + contract_cols(grad_right, second_weight)).astype(
            jnp.bfloat16
        ),
        "mp",
        scatter_dimension=0,
        tiled=True,
    ).astype(jnp.float32)
    grad_middle = cotangent.astype(jnp.float32) + norm_back(middle, scale_three, grad_second_in)
    grad_branch = grad_middle.astype(jnp.bfloat16)
    grad_mixed = contract_cols(grad_branch, out_weight)
    grad_sel = (grad_mixed * normal_att).astype(jnp.bfloat16)
    grad_attended = norm_back(attended, scale_two, grad_mixed * select).reshape(count, heads, HEAD)
    carried_grads = carried_back(grad_attended)
    end_grads = carried_in((carry_factor, carried_grads[1]), "mp", combine, identity)
    grad_queries, grad_keys, grad_values = local_back((grad_attended, end_grads[1]))
    grad_query_pre, grad_key_pre = feature_back((grad_queries + carried_grads[0], grad_keys))
    grad_query_pre = grad_query_pre.astype(jnp.bfloat16)
    grad_key_pre = grad_key_pre.astype(jnp.bfloat16)
    grad_value_rows = grad_values.reshape(count, width).astype(jnp.bfloat16)
    grad_normed = (
        contract_cols(grad_query_pre, query_weight)
        + contract_cols(grad_key_pre, key_weight)
        + contract_cols(grad_value_rows, value_weight)
        + contract_cols(grad_sel, select_weight)
    )
    grad_hidden = (grad_middle + norm_back(hidden, scale_one, grad_normed)).astype(jnp.bfloat16)
    data_part = (
        lax.psum_scatter(
            contract_rows(normed, grad_query_pre).astype(jnp.bfloat16),
            "dp",
            scatter_dimension=0,
            tiled=True,
        ).astype(jnp.float32),
        lax.psum_scatter(
            contract_rows(normed, grad_key_pre).astype(jnp.bfloat16),
            "dp",
            scatter_dimension=0,
            tiled=True,
        ).astype(jnp.float32),
        lax.psum_scatter(
            contract_rows(normed, grad_value_rows).astype(jnp.bfloat16),
            "dp",
            scatter_dimension=0,
            tiled=True,
        ).astype(jnp.float32),
        lax.psum_scatter(
            contract_rows(normed, grad_sel).astype(jnp.bfloat16),
            "dp",
            scatter_dimension=0,
            tiled=True,
        ).astype(jnp.float32),
        lax.psum_scatter(
            contract_rows(mixed, grad_branch).astype(jnp.bfloat16),
            "dp",
            scatter_dimension=0,
            tiled=True,
        ).astype(jnp.float32),
        lax.psum_scatter(
            first_local.astype(jnp.bfloat16), "dp", scatter_dimension=0, tiled=True
        ).astype(jnp.float32),
        lax.psum_scatter(
            second_local.astype(jnp.bfloat16), "dp", scatter_dimension=0, tiled=True
        ).astype(jnp.float32),
        lax.psum_scatter(
            down_local.astype(jnp.bfloat16), "dp", scatter_dimension=0, tiled=True
        ).astype(jnp.float32),
    )
    model_part = (
        lax.psum_scatter(
            data_part[0].astype(jnp.bfloat16), "mp", scatter_dimension=1, tiled=True
        ).astype(jnp.float32),
        lax.psum_scatter(
            data_part[1].astype(jnp.bfloat16), "mp", scatter_dimension=1, tiled=True
        ).astype(jnp.float32),
        lax.psum_scatter(
            data_part[2].astype(jnp.bfloat16), "mp", scatter_dimension=1, tiled=True
        ).astype(jnp.float32),
        lax.psum_scatter(
            data_part[3].astype(jnp.bfloat16), "mp", scatter_dimension=1, tiled=True
        ).astype(jnp.float32),
        lax.psum_scatter(
            data_part[4].astype(jnp.bfloat16), "mp", scatter_dimension=1, tiled=True
        ).astype(jnp.float32),
    )
    reduced = (
        model_part[0],
        model_part[1],
        model_part[2],
        model_part[3],
        model_part[4],
        data_part[5],
        data_part[6],
        data_part[7],
    )
    return (
        output,
        grad_hidden,
        reduced[0],
        reduced[1],
        reduced[2],
        reduced[3],
        reduced[4],
        reduced[5],
        reduced[6],
        jnp.transpose(reduced[7]),
    )


def solution(mesh):
    in_specs = (
        P(("dp", "mp"), None),
        P(),
        P(),
        P(),
        P(),
        P(),
        P(None, "mp"),
        P(None, "mp"),
        P("mp", None),
        P(),
        P("dp", None),
        P(("dp", "mp"), None),
    )
    out_specs = (
        P(("dp", "mp"), None),
        P(("dp", "mp"), None),
        P("dp", "mp"),
        P("dp", "mp"),
        P("dp", "mp"),
        P("dp", "mp"),
        P("dp", "mp"),
        P("dp", "mp"),
        P("dp", "mp"),
        P("mp", "dp"),
    )
    return jax.shard_map(
        per_device, mesh=mesh, in_specs=in_specs, out_specs=out_specs, check_vma=False
    )
```

profile of v0, /device:TPU:12, one launch (start us, length us, event | category | flops | bytes accessed | tf_op | source)
XLA Modules:
  0.0 1122.8 jit_solution(14144861008531119652)
XLA Ops:
  12.2 3.9 copy.78
  19.5 6.7 fusion.95
  26.2 6.1 fusion.59
  32.3 5.3 copy.81
  37.8 8.4 fusion.60
  46.1 5.3 copy.79
  51.5 2.9 multiply_cosine_fusion
  54.5 10.0 broadcast_multiply_fusion.2
  65.2 18.4 %fusion.79 = bf16[8,256,128]{2,1,0:T(8,128)(2,1)} fusion(f32[1024,8,128]{0,2,1:T(8,128)} %bitcast.150, f32[1024,8]{0,1:T(8,128)S(1)} %get-tuple-element.284, f32[1024,8,128]{2,0,1:T(8,128)} %get-tuple-element.270, f32[1024,8,128]{2,0,1:T(8,128)} %get-tuple-element.269), kind=kOutput, calls=%fused_computation.128 | convolution fusion | flops 3225681920 | bytes 13139968 | tf_op jit(solution)/shard_map/jvp(shd,she->hde)/dot_general | solution.py:155
  90.2 4.9 all-reduce
  95.2 33.7 %fusion.65 = f32[8,1024,1024]{2,1,0:T(8,128)} fusion(f32[1024,8,128]{2,0,1:T(8,128)} %get-tuple-element.270, f32[1024,8,128]{2,0,1:T(8,128)} %get-tuple-element.269, f32[1024,8,128]{2,0,1:T(8,128)} %get-tuple-element.271, f32[1024,8,128]{2,0,1:T(8,128)} %get-tuple-element.272), kind=kOutput, calls=%fused_computation.109 | convolution fusion | flops 25773998080 | bytes 50331648 | tf_op jit(solution)/shard_map/jvp(thd,shd->hts)/dot_general | solution.py:153
  128.9 5.0 while.29
  133.9 14.7 %fusion.66 = f32[8,128,1024]{2,1,0:T(8,128)} fusion(f32[8,256,128]{2,1,0:T(8,128)} %get-tuple-element.188, f32[1024,8,128]{2,0,1:T(8,128)} %get-tuple-element.271, f32[1024,8,128]{2,0,1:T(8,128)} %get-tuple-element.272), kind=kOutput, calls=%fused_computation.110 | convolution fusion | flops 3223322624 | bytes 13631488 | tf_op jit(solution)/shard_map/jvp(thd,hde->the)/dot_general | solution.py:161
  148.6 46.3 %multiply_reduce_fusion.1 = (f32[1024]{0:T(1024)S(1)}, f32[1024,8,128]{0,2,1:T(8,128)S(1)}) fusion(f32[8,128,1024]{2,1,0:T(8,128)} %fusion.66, f32[1024,8]{0,1:T(8,128)S(1)} %get-tuple-element.283, f32[1024,8,128]{0,2,1:T(8,128)} %bitcast.151, f32[8,1024,1024]{2,1,0:T(8,128)} %fusion.65, f32[1024,1024]{1,0:T(8,128)} %convert_maximum_fusion, ...), kind=kOutput, calls=%fused_computation.95 | convolution fusion | flops 12914260992 | bytes 51417120 | tf_op jit(solution)/shard_map/jvp(hts,she->the)/dot_general | solution.py:154
  195.0 7.6 multiply_convert_fusion.5
  210.1 56.3 %all-gather.8.cloned.1.call-done = bf16[2048,1024]{0,1:T(8,128)(2,1)} async-done(((bf16[1024,1024]{0,1:T(8,128)(2,1)}), bf16[2048,1024]{0,1:T(8,128)(2,1)}) %all-gather.8.cloned.1.call-update) | async-done | bytes 4194320 | tf_op jit(solution)/shard_map/all_gather | solution.py:191
  266.4 12.7 %fusion.111 = f32[2048,1408]{1,0:T(8,128)} fusion(bf16[2048,1024]{0,1:T(8,128)(2,1)} %all-gather.8.cloned.1.call-done, bf16[1024,1408]{1,0:T(8,128)(2,1)} %param.22), kind=kOutput, calls=%fused_computation.178 | convolution fusion | flops 5905580032 | bytes 18612224 | tf_op jit(solution)/shard_map/dot_general | solution.py:62
  279.2 9.6 fusion.112
  288.7 36.0 %all-gather.10.cloned.1.call-done = bf16[2048,1024]{1,0:T(8,128)(2,1)} async-done(((bf16[1024,1024]{1,0:T(8,128)(2,1)}), bf16[2048,1024]{1,0:T(8,128)(2,1)}) %all-gather.10.cloned.1.call-update) | async-done | bytes 4194320 | tf_op jit(solution)/shard_map/all_gather | solution.py:199
  324.8 15.8 %multiply_convert_fusion = (bf16[2048,1408]{1,0:T(8,128)(2,1)}, bf16[2048,1408]{1,0:T(8,128)(2,1)}, bf16[2048,1408]{1,0:T(8,128)(2,1)}) fusion(f32[2048,1408]{1,0:T(8,128)} %fusion.111, f32[2048,1408]{1,0:T(8,128)} %fusion.112, bf16[2048,1024]{1,0:T(8,128)(2,1)} %all-gather.10.cloned.1.call-done, bf16[1408,1024]{1,0:T(8,128)(2,1)S(1)} %copy-done), kind=kOutput, calls=%fused_computation.28 | convolution fusion | flops 5922881536 | bytes 47448064 | tf_op jit(solution)/shard_map/dot_general | solution.py:72
  340.6 9.7 fusion.113
  350.3 8.4 add_convert_fusion
  358.8 11.0 convolution_convert_fusion.3
  372.8 40.4 %reduce-scatter.20.cloned.1.call-done = bf16[1024,1024]{0,1:T(8,128)(2,1)} async-done(((bf16[2048,1024]{0,1:T(8,128)(2,1)}), bf16[1024,1024]{0,1:T(8,128)(2,1)}) %reduce-scatter.20.cloned.1.call-update) | async-done | bytes 2097168 | tf_op jit(solution)/shard_map/reduce_scatter | solution.py:206
  413.2 3.4 fusion.33
  416.7 53.1 %reduce-scatter.18.cloned.1.call-done = bf16[1024,1024]{0,1:T(8,128)(2,1)} async-done(((bf16[2048,1024]{0,1:T(8,128)(2,1)}), bf16[1024,1024]{0,1:T(8,128)(2,1)}) %reduce-scatter.18.cloned.1.call-update) | async-done | bytes 2097168 | tf_op jit(solution)/shard_map/reduce_scatter | solution.py:195
  469.8 6.7 fusion.32
  476.6 4.4 fusion.55
  481.0 4.8 multiply_convert_fusion.3
  487.8 16.7 %fusion.76 = bf16[8,256,128]{2,1,0:T(8,128)(2,1)} fusion(f32[1024,8,128]{0,2,1:T(8,128)S(1)} %bitcast.146, f32[1024,8]{0,1:T(8,128)S(1)} %get-tuple-element.283, f32[1024,8,128]{2,0,1:T(8,128)} %get-tuple-element.271, f32[1024,8,128]{2,0,1:T(8,128)} %get-tuple-element.272), kind=kOutput, calls=%fused_computation.127 | convolution fusion | flops 3224633344 | bytes 13139968 | tf_op jit(solution)/shard_map/transpose(jvp(thd,hde->the))/dot_general | solution.py:161
  504.5 9.7 fusion.67
  517.2 11.2 %convolution_convert_fusion.2 = bf16[1024,1408]{1,0:T(8,128)(2,1)} fusion(bf16[2048,1024]{0,1:T(8,128)(2,1)} %all-gather.8.cloned.1.call-done, bf16[2048,1408]{1,0:T(8,128)(2,1)} %get-tuple-element.262), kind=kOutput, calls=%fused_computation.113 | convolution fusion | flops 5907021824 | bytes 12845056 | tf_op jit(solution)/shard_map/dot_general | solution.py:66
  528.5 11.7 %convolution_convert_fusion.1 = bf16[1024,1408]{1,0:T(8,128)(2,1)} fusion(bf16[2048,1024]{0,1:T(8,128)(2,1)} %all-gather.8.cloned.1.call-done, bf16[2048,1408]{1,0:T(8,128)(2,1)} %get-tuple-element.260), kind=kOutput, calls=%fused_computation.112 | convolution fusion | flops 5907021824 | bytes 12845056 | tf_op jit(solution)/shard_map/dot_general | solution.py:66
  540.3 6.9 convolution_convert_fusion.4
  547.3 5.4 convolution_convert_fusion.5
  552.7 31.8 %fusion.114 = f32[8,1024,1024]{2,1,0:T(8,128)} fusion(f32[8,128,1024]{2,1,0:T(8,128)} %bitcast.147, f32[1024,8,128]{0,2,1:T(8,128)} %bitcast.152), kind=kOutput, calls=%fused_computation.181 | convolution fusion | flops 12884901888 | bytes 41943040 | tf_op jit(solution)/shard_map/transpose(jvp(hts,she->the))/dot_general | solution.py:154
  584.5 42.3 %fusion.9 = f32[8,1024,256]{2,1,0:T(8,128)} fusion(f32[8,1024,1024]{2,1,0:T(8,128)} %fusion.114, f32[1024,1024]{1,0:T(8,128)} %convert_maximum_fusion, f32[8]{0:T(128)S(1)} %copy-done.32, pred[1024,1024]{1,0:T(8,128)(4,1)S(1)} %copy-done.14, f32[1024,8,128]{2,0,1:T(8,128)} %get-tuple-element.270, f32[1024,8,128]{2,0,1:T(8,128)} %get-tuple-element.269), kind=kOutput, calls=%fused_computation.11 | convolution fusion | flops 25797066752 | bytes 55574560 | tf_op jit(solution)/shard_map/transpose(jvp(thd,shd->hts))/dot_general | solution.py:153
  626.9 12.3 %add_bitcast_fusion = f32[1024,8,256]{2,0,1:T(8,128)} fusion(f32[8,1024,256]{2,1,0:T(8,128)} %fusion.9, f32[8,256,128]{2,1,0:T(8,128)S(1)} %copy-done.11, f32[1024,8,128]{0,2,1:T(8,128)} %bitcast.148, f32[1024,8]{0,1:T(8,128)S(1)} %get-tuple-element.283), kind=kOutput, calls=%fused_computation.35 | convolution fusion | flops 3224371200 | bytes 22052864 | tf_op jit(solution)/shard_map/transpose(jvp(thd,hde->the))/dot_general | solution.py:161
  639.2 65.5 %fusion.7 = f32[8,1024,256]{2,1,0:T(8,128)} fusion(f32[8,1024,1024]{2,1,0:T(8,128)} %fusion.114, f32[1024,1024]{1,0:T(8,128)} %convert_maximum_fusion, f32[8]{0:T(128)S(1)} %copy-done.32, pred[1024,1024]{1,0:T(8,128)(4,1)S(1)} %copy-done.14, f32[1024,8,128]{2,0,1:T(8,128)} %get-tuple-element.271, f32[1024,8,128]{2,0,1:T(8,128)} %get-tuple-element.272), kind=kOutput, calls=%fused_computation.10 | convolution fusion | flops 25797066752 | bytes 55574560 | tf_op jit(solution)/shard_map/transpose(jvp(thd,shd->hts))/dot_general | solution.py:153
  705.7 12.0 %bitcast_add_fusion = f32[1024,8,256]{2,0,1:T(8,128)S(1)} fusion(f32[8,1024,256]{2,1,0:T(8,128)} %fusion.7, f32[1024,8]{0,1:T(8,128)S(1)} %copy-done.28, f32[8,256,128]{2,1,0:T(8,128)S(1)} %get-tuple-element.189, f32[1024,8,128]{0,2,1:T(8,128)} %bitcast.153), kind=kOutput, calls=%fused_computation.33 | convolution fusion | flops 3225419776 | bytes 22052864 | tf_op jit(solution)/shard_map/transpose(jvp(shd,she->hde))/dot_general | solution.py:155
  717.6 6.5 fusion.47
  724.1 5.4 copy.95
  729.6 5.3 fusion.36
  736.2 3.7 convolution_convert_fusion.8
  740.0 5.7 copy.101
  745.6 14.1 %fusion.27 = f32[8,128,1024]{2,1,0:T(8,128)} fusion(f32[8,256,128]{2,1,0:T(8,128)S(1)} %get-tuple-element.189, f32[1024,8]{0,1:T(8,128)S(1)} %copy-done.28, f32[1024,8,128]{2,0,1:T(8,128)} %get-tuple-element.270, f32[1024,8,128]{2,0,1:T(8,128)} %get-tuple-element.269), kind=kOutput, calls=%fused_computation.42 | convolution fusion | flops 3225419776 | bytes 13664256 | tf_op jit(solution)/shard_map/transpose(jvp(shd,she->hde))/dot_general | solution.py:155
  762.9 3.7 convolution_convert_fusion.7
  766.7 32.4 %add_convert_fusion.1 = bf16[8,128,1024]{2,1,0:T(8,128)(2,1)S(1)} fusion(f32[8,128,1024]{2,1,0:T(8,128)} %fusion.27, f32[8,128,1024]{2,1,0:T(8,128)} %bitcast.149, f32[8,1024,1024]{2,1,0:T(8,128)} %fusion.65, f32[1024,1024]{1,0:T(8,128)} %convert_maximum_fusion, f32[8]{0:T(128)S(1)} %copy-done.32, pred[1024,1024]{1,0:T(8,128)(4,1)} %fusion.62), kind=kOutput, calls=%fused_computation.90 | convolution fusion | flops 12912164864 | bytes 49283104 | tf_op jit(solution)/shard_map/transpose(jvp(hts,she->the))/dot_general | solution.py:154
  800.4 3.8 convolution_convert_fusion.6
  809.9 4.0 copy.103
  814.0 6.7 fusion.117
  820.7 40.2 %reduce-scatter.38.cloned.1.call-done = bf16[64,1024]{1,0:T(8,128)(2,1)} async-done(((bf16[1024,1024]{1,0:T(8,128)(2,1)}), bf16[64,1024]{1,0:T(8,128)(2,1)}) %reduce-scatter.38.cloned.1.call-update) | async-done | bytes 131088 | tf_op jit(solution)/shard_map/reduce_scatter | solution.py:258
  861.1 6.6 fusion.115
  867.7 57.8 %reduce-scatter.22.cloned.1.call-done = bf16[64,1024]{1,0:T(8,128)(2,1)} async-done(((bf16[1024,1024]{1,0:T(8,128)(2,1)}), bf16[64,1024]{1,0:T(8,128)(2,1)}) %reduce-scatter.22.cloned.1.call-update) | async-done | bytes 131088 | tf_op jit(solution)/shard_map/reduce_scatter | solution.py:234
  925.6 6.6 fusion.116
  932.1 57.7 %reduce-scatter.26.cloned.1.call-done = bf16[64,1024]{1,0:T(8,128)(2,1)} async-done(((bf16[1024,1024]{1,0:T(8,128)(2,1)}), bf16[64,1024]{1,0:T(8,128)(2,1)}) %reduce-scatter.26.cloned.1.call-update) | async-done | bytes 131088 | tf_op jit(solution)/shard_map/reduce_scatter | solution.py:240
  989.9 10.4 fusion.46
  1000.3 54.2 %reduce-scatter.30.cloned.1.call-done = bf16[64,1024]{1,0:T(8,128)(2,1)} async-done(((bf16[1024,1024]{1,0:T(8,128)(2,1)}), bf16[64,1024]{1,0:T(8,128)(2,1)}) %reduce-scatter.30.cloned.1.call-update) | async-done | bytes 131088 | tf_op jit(solution)/shard_map/reduce_scatter | solution.py:246
  1054.6 6.8 fusion.45
  1061.4 3.9 copy.104
  1066.8 10.6 reduce-scatter.40.cloned.1.call-done
  1078.9 10.8 reduce-scatter.24.cloned.1.call-done
  1091.3 10.8 reduce-scatter.28.cloned.1.call-done
  1103.6 11.0 reduce-scatter.32.cloned.1.call-done
  (178 shorter events, 54.1 us)
Async XLA Ops:
  7.2 317.6 %copy-start = (bf16[1408,1024]{1,0:T(8,128)(2,1)S(1)}, bf16[1408,1024]{1,0:T(8,128)(2,1)}, u32[]{:S(2)}) copy-start(bf16[1408,1024]{1,0:T(8,128)(2,1)} %param.24) | copy-start | bytes 8650756
  7.2 121.7 %all-gather.12.cloned.1.call-start = ((), (), s32[]{:S(2)}) async-start(), calls=%async_computation.31 | async-start | bytes 1572864 | tf_op jit(solution)/shard_map/all_gather | solution.py:16
  18.8 176.2 %copy-start.29 = (f32[1024]{0:T(1024)}, f32[1024]{0:T(1024)S(1)}, u32[]{:S(2)}) copy-start(f32[1024]{0:T(1024)S(1)} %get-tuple-element.278) | copy-start | bytes 12292
  19.5 6.7 copy-start.6
  19.5 6.7 copy-start.38
  46.1 5.3 copy-start.34
  51.5 97.1 %copy-start.31 = (f32[8]{0:T(128)}, f32[8]{0:T(128)S(1)}, u32[]{:S(2)}) copy-start(f32[8]{0:T(128)S(1)} %get-tuple-element.285) | copy-start | bytes 100
  54.5 10.0 copy-start.20
  64.5 0.6 copy-start.27
  83.6 5.1 copy-start.41
  83.6 182.8 %all-gather.8.cloned.1.call-start = ((), (), s32[]{:S(2)}) async-start(), calls=%async_computation.15 | async-start | bytes 6291456 | tf_op jit(solution)/shard_map/all_gather | solution.py:191
  133.9 14.7 %copy-start.39 = (bf16[2,8]{1,0:T(2,128)(2,1)}, bf16[2,8]{1,0:T(2,128)(2,1)S(1)}, u32[]{:S(2)}) copy-start(bf16[2,8]{1,0:T(2,128)(2,1)S(1)} %get-tuple-element.487) | copy-start | bytes 100
  148.6 46.4 %copy-start.7 = (bf16[1024,1024]{0,1:T(8,128)(2,1)S(1)}, bf16[1024,1024]{0,1:T(8,128)(2,1)}, u32[]{:S(2)}) copy-start(bf16[1024,1024]{0,1:T(8,128)(2,1)} %copy.78) | copy-start | bytes 6291460
  194.9 7.7 copy-start.2
  195.0 7.6 copy-start.17
  202.6 2.7 copy-start.19
  205.4 2.0 copy-start.13
  209.3 115.4 %all-gather.10.cloned.1.call-start = ((), (), s32[]{:S(2)}) async-start(), calls=%async_computation.17 | async-start | bytes 6291456 | tf_op jit(solution)/shard_map/all_gather | solution.py:199
  210.1 203.2 %reduce-scatter.20.cloned.1.call-start = ((), (), s32[]{:S(2)}) async-start(), calls=%async_computation.18 | async-start | bytes 6291456 | tf_op jit(solution)/shard_map/reduce_scatter | solution.py:206
  266.4 12.7 %copy-start.35 = (bf16[2048,1024]{0,1:T(8,128)(2,1)S(1)}, bf16[2048,1024]{0,1:T(8,128)(2,1)}, u32[]{:S(2)}) copy-start(bf16[2048,1024]{0,1:T(8,128)(2,1)} %all-gather.8.cloned.1.call-done) | copy-start | bytes 12582916
  266.4 12.7 %copy-start.36 = (bf16[1024,1408]{1,0:T(8,128)(2,1)S(1)}, bf16[1024,1408]{1,0:T(8,128)(2,1)}, u32[]{:S(2)}) copy-start(bf16[1024,1408]{1,0:T(8,128)(2,1)} %param.23) | copy-start | bytes 8650756
  340.5 9.8 copy-start.15
  340.6 9.8 copy-start.37
  358.8 111.0 %reduce-scatter.18.cloned.1.call-start = ((), (), s32[]{:S(2)}) async-start(), calls=%async_computation.16 | async-start | bytes 6291456 | tf_op jit(solution)/shard_map/reduce_scatter | solution.py:195
  369.9 334.9 %all-gather.14.cloned.1.call-start = ((), (), s32[]{:S(2)}) async-start(), calls=%async_computation.32 | async-start | bytes 1572864 | tf_op jit(solution)/shard_map/all_gather | solution.py:41
  469.8 6.8 copy-start.3
  469.8 6.8 copy-start.5
  469.8 6.8 copy-start.18
  476.6 4.5 copy-start.12
  485.8 2.0 copy-start.4
  504.5 299.8 %reduce-scatter.46.cloned.1.call-start = ((), (), s32[]{:S(2)}) async-start(), calls=%async_computation.33 | async-start | bytes 3063808
  517.2 289.4 %reduce-scatter.42.cloned.1.call-start = ((), (), s32[]{:S(2)}) async-start(), calls=%async_computation.29 | async-start | bytes 3063808 | tf_op jit(solution)/shard_map/reduce_scatter | solution.py:264
  528.5 279.8 %reduce-scatter.44.cloned.1.call-start = ((), (), s32[]{:S(2)}) async-start(), calls=%async_computation.30 | async-start | bytes 3063808 | tf_op jit(solution)/shard_map/reduce_scatter | solution.py:267
  540.3 7.0 copy-start.8
  540.3 7.0 copy-start.30
  540.3 273.6 %reduce-scatter.34.cloned.1.call-start = ((), (), s32[]{:S(2)}) async-start(), calls=%async_computation.25 | async-start | bytes 2228224 | tf_op jit(solution)/shard_map/reduce_scatter | solution.py:252
  552.7 31.8 %copy-start.14 = (pred[1024,1024]{1,0:T(8,128)(4,1)S(1)}, pred[1024,1024]{1,0:T(8,128)(4,1)}, u32[]{:S(2)}) copy-start(pred[1024,1024]{1,0:T(8,128)(4,1)} %fusion.62) | copy-start | bytes 3145732
  552.7 31.8 %copy-start.32 = (f32[8]{0:T(128)S(1)}, f32[8]{0:T(128)}, u32[]{:S(2)}) copy-start(f32[8]{0:T(128)} %copy-done.31) | copy-start | bytes 100
  584.5 42.4 %copy-start.11 = (f32[8,256,128]{2,1,0:T(8,128)S(1)}, f32[8,256,128]{2,1,0:T(8,128)}, u32[]{:S(2)}) copy-start(f32[8,256,128]{2,1,0:T(8,128)} %get-tuple-element.188) | copy-start | bytes 3145732
  626.8 234.0 %reduce-scatter.38.cloned.1.call-start = ((), (), s32[]{:S(2)}) async-start(), calls=%async_computation.27 | async-start | bytes 2228224 | tf_op jit(solution)/shard_map/reduce_scatter | solution.py:258
  639.2 65.7 %copy-start.40 = (bf16[2,8]{1,0:T(2,128)(2,1)S(1)}, bf16[2,8]{1,0:T(2,128)(2,1)}, u32[]{:S(2)}) copy-start(bf16[2,8]{1,0:T(2,128)(2,1)} %copy-done.39) | copy-start | bytes 100
  704.7 220.7 %reduce-scatter.22.cloned.1.call-start = ((), (), s32[]{:S(2)}) async-start(), calls=%async_computation.19 | async-start | bytes 2228224 | tf_op jit(solution)/shard_map/reduce_scatter | solution.py:234
  704.9 0.8 copy-start.28
  705.7 12.0 %copy-start.21 = (f32[1024,128]{1,0:T(8,128)S(1)}, f32[1024,128]{1,0:T(8,128)}, u32[]{:S(2)}) copy-start(f32[1024,128]{1,0:T(8,128)} %copy-done.20) | copy-start | bytes 1572868
  705.7 12.0 %copy-start.22 = (f32[1024,128]{1,0:T(8,128)S(1)}, f32[1024,128]{1,0:T(8,128)}, u32[]{:S(2)}) copy-start(f32[1024,128]{1,0:T(8,128)} %get-tuple-element.276) | copy-start | bytes 1572868
  729.6 6.7 copy-start.9
  734.9 1.3 copy-start.25
  739.9 249.9 %reduce-scatter.26.cloned.1.call-start = ((), (), s32[]{:S(2)}) async-start(), calls=%async_computation.21 | async-start | bytes 2228224 | tf_op jit(solution)/shard_map/reduce_scatter | solution.py:240
  745.6 14.1 %copy-start.16 = (f32[1024,8,128]{0,2,1:T(8,128)S(1)}, f32[1024,8,128]{0,2,1:T(8,128)}, u32[]{:S(2)}) copy-start(f32[1024,8,128]{0,2,1:T(8,128)} %copy.101) | copy-start | bytes 12582916
  745.6 14.1 %copy-start.23 = (f32[1024,1024]{0,1:T(8,128)S(1)}, f32[1024,1024]{0,1:T(8,128)}, u32[]{:S(2)}) copy-start(f32[1024,1024]{0,1:T(8,128)} %get-tuple-element.288) | copy-start | bytes 12582916
  759.7 3.1 copy-start.10
  761.5 1.4 copy-start.26
  766.6 287.9 %reduce-scatter.30.cloned.1.call-start = ((), (), s32[]{:S(2)}) async-start(), calls=%async_computation.23 | async-start | bytes 2228224 | tf_op jit(solution)/shard_map/reduce_scatter | solution.py:246
  799.1 1.3 copy-start.24
  804.2 261.1 %reduce-scatter.36.cloned.1.call-start = ((), (), s32[]{:S(2)}) async-start(), calls=%async_computation.26 | async-start | bytes 196608 | tf_op jit(solution)/shard_map/reduce_scatter | solution.py:284
  814.0 263.5 %reduce-scatter.40.cloned.1.call-start = ((), (), s32[]{:S(2)}) async-start(), calls=%async_computation.28 | async-start | bytes 196608 | tf_op jit(solution)/shard_map/reduce_scatter | solution.py:287
  860.9 228.9 %reduce-scatter.24.cloned.1.call-start = ((), (), s32[]{:S(2)}) async-start(), calls=%async_computation.20 | async-start | bytes 196608 | tf_op jit(solution)/shard_map/reduce_scatter | solution.py:275
  925.5 176.6 %reduce-scatter.28.cloned.1.call-start = ((), (), s32[]{:S(2)}) async-start(), calls=%async_computation.22 | async-start | bytes 196608 | tf_op jit(solution)/shard_map/reduce_scatter | solution.py:278
  989.8 64.7 %copy-start.33 = (f32[1024]{0:T(1024)S(1)}, f32[1024]{0:T(1024)}, u32[]{:S(2)}) copy-start(f32[1024]{0:T(1024)} %get-tuple-element.277) | copy-start | bytes 12292
  989.9 124.7 %reduce-scatter.32.cloned.1.call-start = ((), (), s32[]{:S(2)}) async-start(), calls=%async_computation.24 | async-start | bytes 196608 | tf_op jit(solution)/shard_map/reduce_scatter | solution.py:281
  1054.5 61.6 %copy-start.1 = (bf16[1408,1024]{1,0:T(8,128)(2,1)S(1)}, bf16[1408,1024]{1,0:T(8,128)(2,1)}, u32[]{:S(2)}) copy-start(bf16[1408,1024]{1,0:T(8,128)(2,1)} %param.24) | copy-start | bytes 8650756
Sparse Core Ops, SparseCore 0:
  83.7 21.5 all-gather.11
  209.5 56.9 all-gather.7
  268.0 56.7 all-gather.9
  358.9 54.2 reduce-scatter.19
  415.5 54.3 reduce-scatter.17
  504.6 21.3 all-gather.13
  529.8 65.6 reduce-scatter.45
  599.7 63.9 reduce-scatter.41
  667.6 64.0 reduce-scatter.43
  735.7 60.7 reduce-scatter.33
  800.3 60.5 reduce-scatter.37
  864.9 60.5 reduce-scatter.21
  929.2 60.5 reduce-scatter.25
  993.9 60.5 reduce-scatter.29
  1056.6 8.4 reduce-scatter.35
  1067.1 10.2 reduce-scatter.39
  1079.5 10.2 reduce-scatter.23
  1091.8 10.2 reduce-scatter.27
  1104.3 10.2 reduce-scatter.31
where the time goes:
time: 1140 us; the launch traced here: 1120 us
  matrix products  530 us (46%)
  waiting for transfers between devices  440 us (39%)
  other arithmetic  77 us (7%)
  local copies, waits for them, and re-layouts  52.6 us (5%)
  between operations  17.3 us (2%)
    dot_general x3, matrix products, local_part(): jnp.einsum('thd,shd->hts', queries, keys, precision=HIGHEST) * decay_table  142 us
    dot_general x3, matrix products, local_part(): result = jnp.einsum('hts,she->the', scores, value_heads, precision=HIGHEST)  111 us
    dot_general x8, matrix products, contract_cols(): lax.dot_general(left, right, (((1,), (1,)), ((), ())), preferred_element_...  68.6 us
    dot_general x8, matrix products, matmul(): return jnp.dot(left, right, preferred_element_type=jnp.float32)  64.8 us
    reduce_scatter x1, waiting for transfers between devices, per_device(): lax.psum_scatter(contract_rows(normed, grad_query_pre).astype(jnp.bfloat1...  57.8 us
    reduce_scatter x1, waiting for transfers between devices, per_device(): lax.psum_scatter(contract_rows(normed, grad_key_pre).astype(jnp.bfloat16)...  57.7 us
    all_gather x1, waiting for transfers between devices, per_device(): gathered = lax.all_gather(second_in, 'mp', axis=0, tiled=True)  56.3 us
    dot_general x8, matrix products, contract_rows(): lax.dot_general(left, right, (((0,), (0,)), ((), ())), preferred_element_...  56.1 us
  transfers between devices with their start and end apart: 19, of which 12 were waited for; matrix products, arithmetic and copies ran while one was open for 38% of the time, Pallas kernels for 0%

commit v1 on v0

v1 whole, which is shorter than its diff:
```python
import functools

import jax
import jax.numpy as jnp
import numpy as np
from jax import lax
from jax.experimental import pallas as pl
from jax.experimental.pallas import tpu as pltpu
from jax.sharding import PartitionSpec as P

HEAD = 128
CHUNK = 256
EPSILON = 1e-06
BF16 = jnp.bfloat16
F32 = jnp.float32
VMEM_LIMIT = 58 * 1024 * 1024


def nn(left, right):
    return jnp.dot(left, right, preferred_element_type=F32)


def nt(left, right):
    return lax.dot_general(left, right, (((1,), (1,)), ((), ())), preferred_element_type=F32)


def scale_of(values):
    return lax.rsqrt(jnp.mean(values * values, axis=-1, keepdims=True) + EPSILON)


def norm_back(values, scale, upstream):
    return scale * upstream - values * (scale * scale * scale) * jnp.mean(
        values * upstream, axis=-1, keepdims=True
    )


def sigmoid(v):
    return 1.0 / (1.0 + jnp.exp(-v))


def featured(pre, cos, sin):
    act = pre * sigmoid(pre)
    return jnp.concatenate([act * cos, act * sin], axis=-1).astype(BF16)


def head_slice(h):
    return slice(h * HEAD, (h + 1) * HEAD)


def row_index(shape):
    return lax.broadcasted_iota(jnp.int32, shape, 0)


def fade_from_start(slope, width):
    return jnp.exp(-slope * (row_index((CHUNK, width)) + 1).astype(F32))


def fade_to_end(slope, width):
    return jnp.exp(-slope * (CHUNK - 1 - row_index((CHUNK, width))).astype(F32))


def decay_table(slope, transposed):
    rows = lax.broadcasted_iota(jnp.int32, (CHUNK, CHUNK), 0)
    cols = lax.broadcasted_iota(jnp.int32, (CHUNK, CHUNK), 1)
    gap = cols - rows if transposed else rows - cols
    return jnp.where(gap >= 0, jnp.exp(-slope * jnp.maximum(gap, 0).astype(F32)), 0.0)


def smem():
    return pl.BlockSpec(memory_space=pltpu.SMEM)


def anywhere():
    return pl.BlockSpec(memory_space=pl.ANY)


def whole_block(shape):
    zeros = (0,) * len(shape)
    return pl.BlockSpec(shape, lambda *_: zeros)


def params(steps=1):
    return pltpu.CompilerParams(
        vmem_limit_bytes=VMEM_LIMIT, dimension_semantics=("arbitrary",) * steps
    )


def cost(flops, arrays):
    moved = sum(int(np.prod(a.shape)) * jnp.dtype(a.dtype).itemsize for a in arrays)
    return pl.CostEstimate(flops=int(flops), bytes_accessed=moved, transcendentals=0)


def struct(shape, dtype=BF16):
    return jax.ShapeDtypeStruct(tuple(shape), dtype)


def chunk_info(lengths, offset, count):
    chunks = count // CHUNK
    ends = jnp.cumsum(lengths)
    starts = ends - lengths
    first = offset + CHUNK * jnp.arange(chunks, dtype=jnp.int32)
    begin = jnp.max(jnp.where(starts[None, :] <= first[:, None], starts[None, :], 0), axis=1)
    base = first - begin
    keep = (base > 0).astype(jnp.int32)
    before = jnp.cumprod(keep)
    after = jnp.concatenate([jnp.cumprod(keep[::-1])[::-1][1:], jnp.ones((1,), jnp.int32)])
    live = jnp.clip(ends[-1] - offset, 0, count)
    return jnp.concatenate([base, keep, before, after, live[None]]).astype(jnp.int32)


def cos_sin_tables(rows):
    freq = 10000.0 ** (-np.arange(HEAD, dtype=np.float64) / HEAD)
    phase = np.arange(rows, dtype=np.float64)[:, None] * freq[None, :]
    return jnp.asarray(np.cos(phase), F32), jnp.asarray(np.sin(phase), F32)


def keys_kernel(chunks, heads, info, slopes, hid, wk, wv, cos, sin, normed_o, turned_o, kpre_o, val_o, st_o, fin_o, state):
    c = pl.program_id(0)

    @pl.when(c == 0)
    def _():
        state[...] = jnp.zeros_like(state)

    x = hid[...].astype(F32)
    normed = (x * scale_of(x)).astype(BF16)
    normed_o[...] = normed
    turned_o[...] = normed.T.reshape(turned_o.shape)
    kpre = nn(normed, wk[...])
    kpre_o[...] = kpre.astype(BF16)
    values = nn(normed, wv[...])
    val_o[...] = values.astype(BF16)
    rows = pl.ds(pl.multiple_of(info[c], CHUNK), CHUNK)
    cs, sn = cos[rows, :], sin[rows, :]
    keep = info[chunks + c].astype(F32)
    for h in range(heads):
        slope = slopes[h]
        key = featured(kpre[:, head_slice(h)], cs, sn)
        faded = (values[:, head_slice(h)] * fade_to_end(slope, HEAD)).astype(BF16)
        old = state[h] * keep
        st_o[0, h] = old.astype(BF16)
        state[h] = jnp.exp(jnp.full((1, 2 * HEAD), -slope * CHUNK, F32)) * old + nn(faded.T, key)
    fin_o[...] = state[...].astype(BF16)


def run_keys(info, slopes, hidden, wk, wv, cos, sin, parts):
    n, d = hidden.shape
    heads, chunks = d // HEAD, n // CHUNK
    turned = (parts // 2, 2, d // parts, n)
    tile = pl.BlockSpec((CHUNK, d), lambda c: (c, 0))
    outs = [
        struct((n, d)),
        struct(turned),
        struct((n, d)),
        struct((n, d)),
        struct((chunks, heads, HEAD, 2 * HEAD)),
        struct((heads, HEAD, 2 * HEAD)),
    ]
    return pl.pallas_call(
        functools.partial(keys_kernel, chunks, heads),
        grid=(chunks,),
        in_specs=[smem(), smem(), tile, whole_block(wk.shape), whole_block(wv.shape), whole_block(cos.shape), whole_block(sin.shape)],
        out_specs=[
            tile,
            pl.BlockSpec(turned[:3] + (CHUNK,), lambda c: (0, 0, 0, c)),
            tile,
            tile,
            pl.BlockSpec((1, heads, HEAD, 2 * HEAD), lambda c: (c, 0, 0, 0)),
            whole_block((heads, HEAD, 2 * HEAD)),
        ],
        out_shape=outs,
        scratch_shapes=[pltpu.VMEM((heads, HEAD, 2 * HEAD), F32)],
        compiler_params=params(),
        cost_estimate=cost(4 * n * d * d, [hidden, wk, wv] + outs),
        name="keys_values_states",
    )(info, slopes, hidden, wk, wv, cos, sin)


def inside_kernel(chunks, heads, info, slopes, normed, wq, ws, kpre, values, st, cos, sin, qpre_o, sel_o, att_o):
    c = pl.program_id(0)
    x = normed[...]
    qpre = nn(x, wq[...])
    qpre_o[...] = qpre.astype(BF16)
    sel_o[...] = nn(x, ws[...]).astype(BF16)
    rows = pl.ds(pl.multiple_of(info[c], CHUNK), CHUNK)
    cs, sn = cos[rows, :], sin[rows, :]
    for h in range(heads):
        slope = slopes[h]
        query = featured(qpre[:, head_slice(h)], cs, sn)
        key = featured(kpre[:, head_slice(h)].astype(F32), cs, sn)
        weights = (nt(query, key) * decay_table(slope, False)).astype(BF16)
        att_o[:, head_slice(h)] = nn(weights, values[:, head_slice(h)]) + fade_from_start(
            slope, HEAD
        ) * nt(query, st[0, h])


def run_inside(info, slopes, normed, wq, ws, kpre, values, st, cos, sin):
    n, d = normed.shape
    heads, chunks = d // HEAD, n // CHUNK
    tile = pl.BlockSpec((CHUNK, d), lambda c: (c, 0))
    outs = [struct((n, d)), struct((n, d)), struct((n, d), F32)]
    return pl.pallas_call(
        functools.partial(inside_kernel, chunks, heads),
        grid=(chunks,),
        in_specs=[
            smem(),
            smem(),
            tile,
            whole_block(wq.shape),
            whole_block(ws.shape),
            tile,
            tile,
            pl.BlockSpec((1, heads, HEAD, 2 * HEAD), lambda c: (c, 0, 0, 0)),
            whole_block(cos.shape),
            whole_block(sin.shape),
        ],
        out_specs=[tile, tile, tile],
        out_shape=outs,
        compiler_params=params(),
        cost_estimate=cost(6 * n * d * d, [normed, wq, ws, kpre, values, st] + outs),
        name="queries_attention",
    )(info, slopes, normed, wq, ws, kpre, values, st, cos, sin)


def mix_kernel(chunks, heads, info, slopes, att, qpre, came, sel, wo, hid, cot, cos, sin, att_o, mixt_o, mid_o, sec_o, sect_o, cott_o, total):
    c = pl.program_id(0)
    rows = pl.ds(pl.multiple_of(info[c], CHUNK), CHUNK)
    cs, sn = cos[rows, :], sin[rows, :]
    reached = info[2 * chunks + c].astype(F32)
    lag = (c * CHUNK).astype(F32)
    alive = (row_index((CHUNK, HEAD)) + c * CHUNK < info[4 * chunks]).astype(F32)
    for h in range(heads):
        slope = slopes[h]
        query = featured(qpre[:, head_slice(h)].astype(F32), cs, sn)
        fade = jnp.exp(-slope * (row_index((CHUNK, HEAD)).astype(F32) + (lag + 1.0))) * reached
        total[:, head_slice(h)] = (att[:, head_slice(h)] + fade * nt(query, came[h])) * alive
    attended = total[...]
    att_o[...] = attended.astype(BF16)
    mixed = (attended * scale_of(attended) * sel[...].astype(F32)).astype(BF16)
    mixt_o[...] = mixed.T.reshape(mixt_o.shape)
    middle = hid[...].astype(F32) + nn(mixed, wo[...])
    mid_o[...] = middle
    second = (middle * scale_of(middle)).astype(BF16)
    sec_o[...] = second
    sect_o[...] = second.T.reshape(sect_o.shape)
    cott_o[...] = cot[...].T.reshape(cott_o.shape)


def run_mix(info, slopes, att, qpre, came, sel, wo, hidden, cot, cos, sin, parts):
    n, d = hidden.shape
    heads, chunks = d // HEAD, n // CHUNK
    turned = (parts // 2, 2, d // parts, n)
    tile = pl.BlockSpec((CHUNK, d), lambda c: (c, 0))
    turned_tile = pl.BlockSpec(turned[:3] + (CHUNK,), lambda c: (0, 0, 0, c))
    outs = [
        struct((n, d)),
        struct(turned),
        struct((n, d), F32),
        struct((n, d)),
        struct(turned),
        struct(turned),
    ]
    return pl.pallas_call(
        functools.partial(mix_kernel, chunks, heads),
        grid=(chunks,),
        in_specs=[
            smem(),
            smem(),
            tile,
            tile,
            whole_block(came.shape),
            tile,
            whole_block(wo.shape),
            tile,
            tile,
            whole_block(cos.shape),
            whole_block(sin.shape),
        ],
        out_specs=[tile, turned_tile, tile, tile, turned_tile, turned_tile],
        out_shape=outs,
        scratch_shapes=[pltpu.VMEM((CHUNK, d), F32)],
        compiler_params=params(),
        cost_estimate=cost(3 * n * d * d, [att, qpre, sel, wo, hidden, cot] + outs),
        name="carried_mixed_middle",
    )(info, slopes, att, qpre, came, sel, wo, hidden, cot, cos, sin)


def sglu_kernel(chunks, heads, peers, plan, first, last, place, info, slopes, *refs):
    refs = list(refs)
    take = lambda k: [refs.pop(0) for _ in range(k)]
    step = pl.program_id(0)
    c = chunks - 1 - step
    (sec, cot) = take(2)
    sources = take(len(plan))
    if not first:
        (term_i, part_i) = take(2)
    if last:
        (mid, sel, att, wo, qpre, cos, sin) = take(7)
    (inner_o, left_o, right_o) = take(3)
    if last:
        (out_o, gmid_o, gbr_o, gsel_o, gatt_o, et_o, e0_o) = take(7)
    else:
        (term_o, part_o) = take(2)
    (w1, w2, wd, sems) = take(4)
    if last:
        (state,) = take(1)

    def copies():
        for i, (which, low, size, slot, row, rows) in enumerate(plan):
            src, dst = sources[i], (w1, w2, wd)[which]
            if low is not None:
                src = src.at[:, pl.ds(low, size)] if which < 2 else src.at[pl.ds(low, size), :]
            if slot is not None:
                dst = dst.at[place[slot]]
                if rows is not None:
                    dst = dst.at[pl.ds(pl.multiple_of(place[row] * rows, rows), rows), :]
            yield pltpu.make_async_copy(src, dst, sems.at[i])

    @pl.when(step == 0)
    def _():
        for copy in copies():
            copy.start()
        if last:
            state[...] = jnp.zeros_like(state)
        for copy in copies():
            copy.wait()

    x, y = sec[...], cot[...]
    term = None if first else term_i[...]
    part = None if first else part_i[...].astype(F32)
    for b in range(peers):
        left = nn(x, w1[b])
        right = nn(x, w2[b])
        inner = (left * right).astype(BF16)
        inner_o[b] = inner
        upstream = nt(y, wd[b])
        grad_left = (upstream * right).astype(BF16)
        grad_right = (upstream * left).astype(BF16)
        left_o[b] = grad_left
        right_o[b] = grad_right
        new_term = nn(inner, wd[b])
        new_part = nt(grad_left, w1[b]) + nt(grad_right, w2[b])
        term = new_term if term is None else term + new_term
        part = new_part if part is None else part + new_part
    if not last:
        term_o[...] = term
        part_o[...] = part
        return
    middle = mid[...]
    out_o[...] = (middle + term).astype(BF16)
    grad_middle = y.astype(F32) + norm_back(middle, scale_of(middle), part)
    gmid_o[...] = grad_middle
    branch = grad_middle.astype(BF16)
    gbr_o[...] = branch
    grad_mixed = nt(branch, wo[...])
    attended = att[...].astype(F32)
    scale = scale_of(attended)
    gsel_o[...] = (grad_mixed * attended * scale).astype(BF16)
    alive = (row_index((CHUNK, 1)) + c * CHUNK < info[4 * chunks]).astype(F32)
    grad_att = norm_back(attended, scale, grad_mixed * sel[...].astype(F32)) * alive
    gatt_o[...] = grad_att.astype(BF16)
    rows = pl.ds(pl.multiple_of(info[c], CHUNK), CHUNK)
    cs, sn = cos[rows, :], sin[rows, :]
    keep = info[chunks + c].astype(F32)
    for h in range(heads):
        slope = slopes[h]
        query = featured(qpre[:, head_slice(h)].astype(F32), cs, sn)
        faded = (grad_att[:, head_slice(h)] * fade_from_start(slope, HEAD)).astype(BF16)
        old = state[h]
        et_o[0, h] = old.astype(BF16)
        state[h] = keep * (
            jnp.exp(jnp.full((1, 2 * HEAD), -slope * CHUNK, F32)) * old + nn(faded.T, query)
        )
    e0_o[...] = state[...].astype(BF16)


def run_sglu(place, info, slopes, second, cot, sources, plan, peers, width, before, after):
    n, d = second.shape
    heads, chunks = d // HEAD, n // CHUNK
    first, last = before is None, after is not None
    tile = pl.BlockSpec((CHUNK, d), lambda s: (chunks - 1 - s, 0))
    inputs = [second, cot] + list(sources)
    specs = [tile, tile] + [anywhere()] * len(sources)
    if not first:
        inputs += list(before)
        specs += [tile, tile]
    if last:
        mid, sel, att, wo, qpre, cos, sin = after
        inputs += [mid, sel, att, wo, qpre, cos, sin]
        specs += [tile, tile, tile, whole_block(wo.shape), tile, whole_block(cos.shape), whole_block(sin.shape)]
    hidden_tile = pl.BlockSpec((peers, CHUNK, width), lambda s: (0, chunks - 1 - s, 0))
    outs = [struct((peers, n, width))] * 3
    out_specs = [hidden_tile] * 3
    scratch = [
        pltpu.VMEM((peers, d, width), BF16),
        pltpu.VMEM((peers, d, width), BF16),
        pltpu.VMEM((peers, width, d), BF16),
        pltpu.SemaphoreType.DMA((len(plan),)),
    ]
    if last:
        outs += [
            struct((n, d)),
            struct((n, d), F32),
            struct((n, d)),
            struct((n, d)),
            struct((n, d)),
            struct((chunks, heads, HEAD, 2 * HEAD)),
            struct((heads, HEAD, 2 * HEAD)),
        ]
        out_specs += [tile] * 5 + [
            pl.BlockSpec((1, heads, HEAD, 2 * HEAD), lambda s: (chunks - 1 - s, 0, 0, 0)),
            whole_block((heads, HEAD, 2 * HEAD)),
        ]
        scratch.append(pltpu.VMEM((heads, HEAD, 2 * HEAD), F32))
    else:
        outs += [struct((n, d), F32), struct((n, d), F32)]
        out_specs += [tile, tile]
    return pl.pallas_call(
        functools.partial(sglu_kernel, chunks, heads, peers, plan, first, last),
        grid=(chunks,),
        in_specs=[smem(), smem(), smem()] + specs,
        out_specs=out_specs,
        out_shape=outs,
        scratch_shapes=scratch,
        compiler_params=params(),
        cost_estimate=cost(12 * n * d * width * peers, inputs + outs),
        name="sglu_last" if last else "sglu_first",
    )(place, info, slopes, *inputs)


def weights_kernel(items, count, added, half, *refs):
    refs = list(refs)
    lefts = refs[:count]
    rights = refs[count : count + len(items)]
    rest = refs[count + len(items) :]
    out = rest[-1]
    for t, which in enumerate(items):
        left = lefts[which][...]
        left = left.reshape(left.shape[0] * left.shape[1], left.shape[2])
        right = rights[t][...]
        total = nn(left, right).reshape(out.shape[1:])
        if added:
            total = total + rest[0][t].astype(F32)
        out[t] = total.astype(BF16)


def run_weights(half, lefts, items, rights, spec, peers, width, received=None):
    pairs, _, rows, n = lefts[0].shape
    shape = (peers, len(items), pairs, rows, width)
    block = pl.BlockSpec((None,) + shape[1:], lambda m, half: (m, 0, 0, 0, 0))
    left_spec = pl.BlockSpec((pairs, None, rows, n), lambda m, half: (0, half[0], 0, 0))
    inputs = list(lefts) + list(rights)
    specs = [left_spec] * len(lefts) + [spec] * len(rights)
    if received is not None:
        inputs.append(received)
        specs.append(block)
    out = struct(shape)
    return pl.pallas_call(
        functools.partial(weights_kernel, tuple(items), len(lefts), received is not None),
        grid_spec=pltpu.PrefetchScalarGridSpec(
            num_scalar_prefetch=1,
            grid=(peers,),
            in_specs=specs,
            out_specs=block,
        ),
        out_shape=out,
        compiler_params=params(),
        cost_estimate=cost(2 * n * pairs * rows * width * len(items) * peers, inputs + [out]),
        name="weight_gradients",
    )(half, *inputs)


def attention_back_kernel(chunks, first_head, info, slopes, qpre, kpre, values, gatt, st, came, et, left, cos, sin, gq_o, gk_o, gv_o):
    pair, c = pl.program_id(0), pl.program_id(1)
    rows = pl.ds(pl.multiple_of(info[c], CHUNK), CHUNK)
    cs, sn = cos[rows, :], sin[rows, :]
    before = info[2 * chunks + c].astype(F32)
    after = info[3 * chunks + c].astype(F32)
    span = CHUNK * c.astype(F32)
    rest = CHUNK * (chunks - 1 - c).astype(F32)
    for h in range(2):
        slope = slopes[first_head + 2 * pair + h]
        cols = head_slice(h)
        qp, kp = qpre[:, cols].astype(F32), kpre[:, cols].astype(F32)
        qs, ks = sigmoid(qp), sigmoid(kp)
        qa, ka = qp * qs, kp * ks
        query = jnp.concatenate([qa * cs, qa * sn], axis=-1).astype(BF16)
        key = jnp.concatenate([ka * cs, ka * sn], axis=-1).astype(BF16)
        value, grad = values[:, cols], gatt[:, cols]
        lane = jnp.zeros((1, 2 * HEAD), F32)
        state = st[0, h].astype(F32) + came[h].astype(F32) * (jnp.exp(lane - slope * span) * before)
        ending = et[0, h].astype(F32) + left[h].astype(F32) * (jnp.exp(lane - slope * rest) * after)
        state, ending = state.astype(BF16), ending.astype(BF16)
        table, turned = decay_table(slope, False), decay_table(slope, True)
        scores_t = (nt(key, query) * turned).astype(BF16)
        slope_s = (nt(grad, value) * table).astype(BF16)
        slope_t = (nt(value, grad) * turned).astype(BF16)
        start = fade_from_start(slope, HEAD)
        end = fade_to_end(slope, HEAD)
        grad_start = (grad.astype(F32) * start).astype(BF16)
        value_end = (value.astype(F32) * end).astype(BF16)
        dq = nn(slope_s, key) + nn(grad_start, state)
        dk = nn(slope_t, query) + nn(value_end, ending)
        dv = nn(scores_t, grad) + end * nt(key, ending)
        gv_o[:, cols] = dv.astype(BF16)
        dq = dq[:, :HEAD] * cs + dq[:, HEAD:] * sn
        dk = dk[:, :HEAD] * cs + dk[:, HEAD:] * sn
        gq_o[:, cols] = (dq * (qs * (1.0 + qp * (1.0 - qs)))).astype(BF16)
        gk_o[:, cols] = (dk * (ks * (1.0 + kp * (1.0 - ks)))).astype(BF16)


def run_attention_back(info, slopes, qpre, kpre, values, gatt, st, came, et, left, cos, sin, first_head, heads):
    n, d = qpre.shape
    chunks = n // CHUNK
    skip = first_head // 2
    tile = pl.BlockSpec((CHUNK, 2 * HEAD), lambda p, c: (c, skip + p))
    out_tile = pl.BlockSpec((CHUNK, 2 * HEAD), lambda p, c: (c, p))
    states = pl.BlockSpec((1, 2, HEAD, 2 * HEAD), lambda p, c: (c, skip + p, 0, 0))
    ends = pl.BlockSpec((2, HEAD, 2 * HEAD), lambda p, c: (skip + p, 0, 0))
    outs = [struct((n, heads * HEAD))] * 3
    return pl.pallas_call(
        functools.partial(attention_back_kernel, chunks, first_head),
        grid=(heads // 2, chunks),
        in_specs=[smem(), smem(), tile, tile, tile, tile, states, ends, states, ends, whole_block(cos.shape), whole_block(sin.shape)],
        out_specs=[out_tile] * 3,
        out_shape=outs,
        compiler_params=params(2),
        cost_estimate=cost(18 * n * 256 * 256 * heads // 2, [qpre, kpre, values, gatt, st, et] + outs),
        name="attention_backward",
    )(info, slopes, qpre, kpre, values, gatt, st, came, et, left, cos, sin)


def input_kernel(count, *refs):
    grads = refs[:count]
    weights = refs[count : 2 * count]
    hid, gmid, out = refs[2 * count :]
    total = None
    for g, w in zip(grads, weights):
        part = nt(g[...], w[...])
        total = part if total is None else total + part
    x = hid[...].astype(F32)
    out[...] = (gmid[...] + norm_back(x, scale_of(x), total)).astype(BF16)


def run_input(grads, weights, hidden, gmid):
    n, d = hidden.shape
    tile = pl.BlockSpec((CHUNK, d), lambda c: (c, 0))
    out = struct((n, d))
    return pl.pallas_call(
        functools.partial(input_kernel, len(grads)),
        grid=(n // CHUNK,),
        in_specs=[pl.BlockSpec((CHUNK, g.shape[1]), lambda c: (c, 0)) for g in grads]
        + [whole_block(w.shape) for w in weights]
        + [tile, tile],
        out_specs=tile,
        out_shape=out,
        compiler_params=params(),
        cost_estimate=cost(8 * n * d * d, list(grads) + list(weights) + [hidden, gmid, out]),
        name="input_gradient",
    )(*grads, *weights, hidden, gmid)


def across(x, axis, flip):
    size = lax.axis_size(axis)
    return lax.ppermute(x, axis, [(i, i ^ flip) for i in range(size)])


def pick(x, index, axis):
    return lax.dynamic_index_in_dim(x, index, axis, keepdims=False)


def plus(*arrays):
    total = arrays[0].astype(F32)
    for a in arrays[1:]:
        total = total + a.astype(F32)
    return total


def reduced(lefts, items, rights, spec, peers, width):
    dp, me = lax.axis_index("dp"), lax.axis_index("mp")
    core = (dp % 2).astype(jnp.int32).reshape(1)
    run = functools.partial(run_weights, lefts=lefts, items=items, rights=rights, spec=spec, peers=peers, width=width)
    if peers != 2:
        halves = [run(jnp.full((1,), k, jnp.int32)) for k in range(2)]
        full = jnp.stack(halves, axis=3)
        full = full.reshape(peers, len(items), -1, full.shape[4], width)
        mine = lax.psum_scatter(full, "dp", scatter_dimension=2, tiled=False)
        return lax.psum_scatter(mine, "mp", scatter_dimension=0, tiled=False).astype(F32)
    sent = run(1 - core)
    total = run(core, received=across(sent, "dp", 1))
    x, z = (dp // 2) % 2, dp // 4
    depth = lax.axis_size("dp") // 4
    total = total.reshape(2, len(items), depth, 2, -1, width)
    half = depth // 2
    upper, lower = total[:, :, :half], total[:, :, half:]
    from_x = across(pick(upper, 1 - x, 3), "dp", 2)
    from_y = across(pick(lower, 1 - me, 0), "mp", 1)
    upper = plus(pick(upper, x, 3), from_x).astype(BF16)
    lower = plus(pick(lower, me, 0), from_y).astype(BF16)
    from_y = across(pick(upper, 1 - me, 0), "mp", 1)
    from_x = across(pick(lower, 1 - x, 2), "dp", 2)
    upper = plus(pick(upper, me, 0), from_y).astype(BF16)
    lower = plus(pick(lower, x, 2), from_x).astype(BF16)
    line = jnp.concatenate([upper, lower], axis=1)
    parts = [pick(line, z, 1)]
    for k in range(1, depth):
        parts.append(across(pick(line, z ^ k, 1), "dp", 4 * k))
    return plus(*parts)


def per_device(
    hidden_in,
    query_weight,
    key_weight,
    value_weight,
    select_weight,
    out_weight,
    first_weight,
    second_weight,
    down_weight,
    decay_slope,
    doc_lengths,
    cotangent,
):
    count, d = hidden_in.shape
    heads, chunks = d // HEAD, count // CHUNK
    peers, parts = lax.axis_size("mp"), lax.axis_size("dp")
    dp, me = lax.axis_index("dp"), lax.axis_index("mp")
    group = count * peers
    units = first_weight.shape[1]
    lengths = doc_lengths[0].astype(jnp.int32)
    info = chunk_info(lengths, me * count, count)
    cos, sin = cos_sin_tables(group // 2)
    slopes = decay_slope

    if units % 128 == 0:
        cut = -(-units // 256) * 128
        ranges = [(0, cut), (cut, units - cut)]
    else:
        ranges = [(0, units)]

    quarter = dp % 4
    place = jnp.stack([me, 1 - me] + [quarter ^ k for k in range(4)]).astype(jnp.int32)
    plans, fetched = [], []
    for low, size in ranges:
        plan, sources = [], []
        if peers == 2:
            for which, weight in enumerate((first_weight, second_weight, down_weight)):
                rows = d // 4 if which < 2 else size // 4
                at = (quarter * rows, low) if which < 2 else (low + quarter * rows, 0)
                extent = (rows, size) if which < 2 else (rows, d)
                mine = lax.dynamic_slice(weight, at, extent)
                one = across(mine, "mp", 1)
                two = across(one, "dp", 2)
                pieces = {0: one, 2: two, 1: across(one, "dp", 1), 3: across(two, "dp", 1)}
                whole = low == 0 and size == units
                plan.append((which, None if whole else low, size, 0, None, None))
                sources.append(weight)
                for k, piece in pieces.items():
                    plan.append((which, None, None, 1, 2 + k, rows))
                    sources.append(piece)
        else:
            for which, weight in enumerate((first_weight, second_weight, down_weight)):
                weight = weight[:, low : low + size] if which < 2 else weight[low : low + size]
                plan.append((which, None, None, None, None, None))
                sources.append(lax.all_gather(weight, "mp"))
        plans.append(tuple(plan))
        fetched.append(sources)

    normed, normed_t, kpre, values, st, final = run_keys(
        info, slopes, hidden_in, key_weight, value_weight, cos, sin, parts
    )
    whole_keep = info[2 * chunks + chunks - 1].astype(F32)
    decay = jnp.exp(-slopes * count)
    if peers == 2:
        came = across(final, "mp", 1)
        came = jnp.where(me == 1, came, jnp.zeros_like(came))
    else:
        finals = lax.all_gather(final, "mp")
        keeps = lax.all_gather(whole_keep.reshape(1), "mp")[:, 0]

        def ahead(k, total):
            new = finals[k].astype(F32) + (keeps[k] * decay)[:, None, None] * total
            return jnp.where(k < me, new, total)

        came = lax.fori_loop(0, peers, ahead, jnp.zeros(final.shape, F32)).astype(BF16)
    qpre, sel, att = run_inside(
        info, slopes, normed, query_weight, select_weight, kpre, values, st, cos, sin
    )
    attended, mixed_t, middle, second, second_t, cot_t = run_mix(
        info, slopes, att, qpre, came, sel, out_weight, hidden_in, cotangent, cos, sin, parts
    )

    before = None
    pieces = []
    for i, (low, size) in enumerate(ranges):
        last = i == len(ranges) - 1
        after = (middle, sel, attended, out_weight, qpre, cos, sin) if last else None
        got = run_sglu(
            place, info, slopes, second, cotangent, fetched[i], plans[i], peers, size, before, after
        )
        inner, grad_left, grad_right = got[:3]
        if last:
            output, grad_middle, grad_branch, grad_sel, grad_att, et, leaving = got[3:]
        else:
            before = got[3:]
        spec = pl.BlockSpec((None, count, size), lambda m, half: (m, 0, 0))
        pieces.append(
            reduced(
                [second_t, cot_t], (0, 0, 1), [grad_left, grad_right, inner], spec, peers, size
            )
        )
    if peers == 2:
        left = across(leaving, "mp", 1)
        left = jnp.where(me == 0, left, jnp.zeros_like(left))
    else:
        leavings = lax.all_gather(leaving, "mp")

        def behind(step, total):
            k = peers - 1 - step
            new = leavings[k].astype(F32) + (keeps[k] * decay)[:, None, None] * total
            return jnp.where(k > me, new, total)

        left = lax.fori_loop(0, peers, behind, jnp.zeros(leaving.shape, F32)).astype(BF16)

    share = d // peers
    wide = pl.BlockSpec((count, share), lambda m, half: (0, m))
    grad_out_sel = reduced(
        [mixed_t, normed_t], (0, 1), [grad_branch, grad_sel], wide, peers, share
    )
    gq, gk, gv = run_attention_back(
        info, slopes, qpre, kpre, values, grad_att, st, came, et, left, cos, sin, 0, heads
    )
    grad_qkv = reduced([normed_t], (0, 0, 0), [gq, gk, gv], wide, peers, share)
    grad_hidden = run_input(
        [gq, gk, gv, grad_sel],
        [query_weight, key_weight, value_weight, select_weight],
        hidden_in,
        grad_middle,
    )
    sglu = pieces[0] if len(pieces) == 1 else jnp.concatenate(pieces, axis=2)
    return (
        output,
        grad_hidden,
        grad_qkv[0],
        grad_qkv[1],
        grad_qkv[2],
        grad_out_sel[1],
        grad_out_sel[0],
        sglu[0],
        sglu[1],
        jnp.transpose(sglu[2]),
    )


def solution(mesh):
    rows = P(("dp", "mp"), None)
    in_specs = (
        rows,
        P(),
        P(),
        P(),
        P(),
        P(),
        P(None, "mp"),
        P(None, "mp"),
        P("mp", None),
        P(),
        P("dp", None),
        rows,
    )
    out_specs = (rows, rows) + (P("dp", "mp"),) * 7 + (P("mp", "dp"),)
    return jax.shard_map(
        per_device, mesh=mesh, in_specs=in_specs, out_specs=out_specs, check_vma=False
    )
```

time: 1140 us -> 452 us (0.40)
  matrix products: 530 us -> 0 us
  waiting for transfers between devices: 440 us -> 123 us
  Pallas kernels: 0 us -> 216 us
  other arithmetic: 77 us -> 14.1 us
  starting transfers between devices: 0.94 us -> 55.8 us
  local copies, waits for them, and re-layouts: 52.6 us -> 32.1 us
  between operations: 17.3 us -> 2.26 us
    dot_general x36 -> x0, matrix products: 530 us -> none  [the longest x3 142 us: local_part(): jnp.einsum('thd,shd->hts', queries, keys, precision=HIGHEST) * decay_table]
    reduce_scatter x14 -> x0, waiting for transfers between devices: 347 us -> none  [the longest x1 57.8 us: per_device(): lax.psum_scatter(contract_rows(normed, grad_query_pre).astype(jnp.bfloat1...]
    pallas_call x0 -> x15, Pallas kernels: none -> 216 us  [the longest x2 73.7 us: run_sglu(): pl.pallas_call(functools.partial(sglu_kernel, chunks, heads, peers, plan,...]
    ppermute x0 -> x58, waiting for transfers between devices: none -> 123 us  [across(): return lax.ppermute(x, axis, [(i, i ^ flip) for i in range(size)])]
    all_gather x4 -> x0, waiting for transfers between devices: 92.4 us -> none  [the longest x1 56.3 us: per_device(): gathered = lax.all_gather(second_in, 'mp', axis=0, tiled=True)]
    ppermute x0 -> x58, starting transfers between devices: none -> 55.8 us  [across(): return lax.ppermute(x, axis, [(i, i ^ flip) for i in range(size)])]
    convert_element_type x18, other arithmetic: 32.2 us -> 8.29 us  [the longest x4 3.3 us: reduced(): lower = plus(pick(lower, me, 0), from_y).astype(BF16)]
    unnamed x94 -> x62, local copies, waits for them, and re-layouts: 30.1 us -> 10.4 us
  transfers between devices with their start and end apart: 19 -> 58, of which waited for: 12 -> 22; matrix products, arithmetic and copies ran while one was open for 38% -> 9% of each run, Pallas kernels for 0% -> 38%
where the time goes in v1:
time: 452 us; the launch traced here: 444 us
  Pallas kernels  216 us (48%)
  waiting for transfers between devices  123 us (27%)
  starting transfers between devices  55.8 us (12%)
  local copies, waits for them, and re-layouts  32.1 us (7%)
  other arithmetic  14.1 us (3%)
    ppermute x58, waiting for transfers between devices, across(): return lax.ppermute(x, axis, [(i, i ^ flip) for i in range(size)])  123 us
    pallas_call x2, Pallas kernels, run_sglu(): pl.pallas_call(functools.partial(sglu_kernel, chunks, heads, peers, plan,...  73.7 us
    pallas_call x8, Pallas kernels, run_weights(): pl.pallas_call(functools.partial(weights_kernel, tuple(items), len(lefts)...  65.8 us
    ppermute x58, starting transfers between devices, across(): return lax.ppermute(x, axis, [(i, i ^ flip) for i in range(size)])  55.8 us
    pallas_call x1, Pallas kernels, run_attention_back(): pl.pallas_call(functools.partial(attention_back_kernel, chunks, first_hea...  21 us
    pallas_call x1, Pallas kernels, run_input(): pl.pallas_call(functools.partial(input_kernel, len(grads)), grid=(n // CH...  16.4 us
    pallas_call x1, Pallas kernels, run_mix(): pl.pallas_call(functools.partial(mix_kernel, chunks, heads), grid=(chunks...  14 us
    pallas_call x1, Pallas kernels, run_inside(): pl.pallas_call(functools.partial(inside_kernel, chunks, heads), grid=(chu...  14 us
  transfers between devices with their start and end apart: 58, of which 22 were waited for; matrix products, arithmetic and copies ran while one was open for 9% of the time, Pallas kernels for 38%

profile of v1, /device:TPU:12, one launch (start us, length us, event | category | flops | bytes accessed | tf_op | source)
XLA Modules:
  0.0 444.2 jit_solution(11680619522460798027)
XLA Ops:
  3.3 1.6 collective-permute-start.17
  7.5 1.6 collective-permute-start.1
  13.4 11.4 %keys_values_states.1 = (bf16[1024,1024]{1,0:T(8,128)(2,1)}, bf16[8,2,64,1024]{3,2,1,0:T(8,128)(2,1)}, bf16[1024,1024]{1,0:T(8,128)(2,1)}, bf16[1024,1024]{1,0:T...) custom-call(s32[17]{0:T(128)} %concatenate.18.info, f32[8]{0:T(128)} %slopes.11, ...), custom_call_target="tpu_custom_call" | custom-call | flops 4294967296 | bytes 17301504 | tf_op jit(solution)/shard_map/keys_values_states/pallas_call | solution.py:158
  24.8 4.4 collective-permute-done.9.refs_13_
  31.0 5.4 %collective-permute-done.1.refs_3_ = bf16[256,640]{1,0:T(8,128)(2,1)} collective-permute-done((bf16[256,640]{1,0:T(8,128)(2,1)S(1)}, bf16[256,640]{1,0:T(8,128)(2,1)}, u32[]{:S(2)}, u32[]{:S(2)}) %collective-permute-start.1) | collective-permute-done | bytes 327712 | tf_op jit(solution)/shard_map/ppermute | solution.py:564
  36.9 6.5 %collective-permute-done.5.refs_8_ = bf16[256,640]{1,0:T(8,128)(2,1)} collective-permute-done((bf16[256,640]{1,0:T(8,128)(2,1)S(1)}, bf16[256,640]{1,0:T(8,128)(2,1)}, u32[]{:S(2)}, u32[]{:S(2)}) %collective-permute-start.5) | collective-permute-done | bytes 327712 | tf_op jit(solution)/shard_map/ppermute | solution.py:564
  43.4 1.5 collective-permute-start.10
  45.4 1.5 collective-permute-start.6
  47.6 14.2 %collective-permute-done.21.refs_13_ = bf16[192,1024]{1,0:T(8,128)(2,1)S(1)} collective-permute-done((bf16[192,1024]{1,0:T(8,128)(2,1)S(1)}, bf16[192,1024]{1,0:T(8,128)(2,1)S(1)}, u32[]{:S(2)}, u32[]{:S(2)}) %collective-permute-start.21) | collective-permute-done | bytes 393248 | tf_op jit(solution)/shard_map/ppermute | solution.py:564
  61.8 1.6 collective-permute-start.14
  65.3 1.5 collective-permute-start.22
  66.8 14.0 %queries_attention.1 = (bf16[1024,1024]{1,0:T(8,128)(2,1)}, bf16[1024,1024]{1,0:T(8,128)(2,1)}, f32[1024,1024]{1,0:T(8,128)}) custom-call(s32[17]{0:T(128)} %concatenate.18.info, f32[8]{0:T(128)} %slopes.11, bf16[1024,1024]{1,0:T(8,128)(2,1)} %get-tuple-element.43.normed, bf16[1024,1024]{1,0:T(8,128)(2,1)} %refs_4_.1, bf16[1024,1024]{1,0:T(8,128)(2,1)} %refs_7_.5, ...), custom_call_target="tpu_custom_call" | custom-call | flops 6442450944 | bytes 20971520 | tf_op jit(solution)/shard_map/queries_attention/pallas_call | solution.py:201
  82.2 8.1 %collective-permute-done.22.refs_14_ = bf16[192,1024]{1,0:T(8,128)(2,1)S(1)} collective-permute-done((bf16[192,1024]{1,0:T(8,128)(2,1)S(1)}, bf16[192,1024]{1,0:T(8,128)(2,1)S(1)}, u32[]{:S(2)}, u32[]{:S(2)}) %collective-permute-start.22) | collective-permute-done | bytes 393248 | tf_op jit(solution)/shard_map/ppermute | solution.py:564
  91.7 14.0 %carried_mixed_middle.1 = (bf16[1024,1024]{1,0:T(8,128)(2,1)}, bf16[8,2,64,1024]{3,2,1,0:T(8,128)(2,1)}, f32[1024,1024]{1,0:T(8,128)}, bf16[1024,1024]{1,0:T(8,1...) custom-call(s32[17]{0:T(128)} %concatenate.18.info, f32[8]{0:T(128)} %slopes.11, ...), custom_call_target="tpu_custom_call" | custom-call | flops 3221225472 | bytes 29360128 | tf_op jit(solution)/shard_map/carried_mixed_middle/pallas_call | solution.py:262
  107.8 33.9 %sglu_first.1 = (bf16[2,1024,768]{2,1,0:T(8,128)(2,1)}, bf16[2,1024,768]{2,1,0:T(8,128)(2,1)}, bf16[2,1024,768]{2,1,0:T(8,128)(2,1)}, f32[1024,1024]{1,0:T(8,128)}, f32[1024,1024]{1,0:T(8,128)}) custom-call(s32[6]{0:T(128)} %stack.27.place, s32[17]{0:T(128)} %concatenate.18.info, f32[8]{0:T(128)} %slopes.11, bf16[1024,1024]{1,0:T(8,128)(2,1)} %get-tuple-element.51.refs_0_, ...), custom_call_target="tpu_custom_call" | custom-call | flops 19327352832 | bytes 35389440 | tf_op jit(solution)/shard_map/sglu_first/pallas_call | solution.py:417
  142.9 39.8 %sglu_last.1 = (bf16[2,1024,640]{2,1,0:T(8,128)(2,1)}, bf16[2,1024,640]{2,1,0:T(8,128)(2,1)}, bf16[2,1024,640]{2,1,0:T(8,128)(2,1)}, bf16[1024,1024]{1,0:T(8,128...) custom-call(s32[6]{0:T(128)} %stack.27.place, ...), custom_call_target="tpu_custom_call" | custom-call | flops 16106127360 | bytes 61865984 | tf_op jit(solution)/shard_map/sglu_last/pallas_call | solution.py:417
  182.7 5.9 %weight_gradients.10 = bf16[2,2,8,64,512]{4,3,2,1,0:T(8,128)(2,1)} custom-call(s32[1]{0:T(128)S(6)} %sub.64.half, bf16[8,2,64,1024]{3,2,1,0:T(8,128)(2,1)} %get-tuple-element.66.refs_0_, bf16[8,2,64,1024]{3,2,1,0:T(8,128)(2,1)} %get-tuple-element.65.refs_0_.refs_1_, bf16[1024,1024]{1,0:T(8,128)(2,1)} %get-tuple-element.67.refs_2_, ...), custom_call_target="tpu_custom_call" | custom-call | flops 2147483648 | bytes 10485760 | tf_op jit(solution)/shard_map/weight_gradients/pallas_call | solution.py:457
  189.3 9.3 %weight_gradients.14 = bf16[2,3,8,64,640]{4,3,2,1,0:T(8,128)(2,1)} custom-call(s32[1]{0:T(128)S(6)} %sub.64.half, bf16[8,2,64,1024]{3,2,1,0:T(8,128)(2,1)} %get-tuple-element.68.refs_0_, bf16[8,2,64,1024]{3,2,1,0:T(8,128)(2,1)} %get-tuple-element.69.refs_1_, bf16[2,1024,640]{2,1,0:T(8,128)(2,1)} %get-tuple-element.73.refs_2_, ...), custom_call_target="tpu_custom_call" | custom-call | flops 4026531840 | bytes 15990784 | tf_op jit(solution)/shard_map/weight_gradients/pallas_call | solution.py:457
  198.7 4.3 collective-permute-done.25
  205.1 6.0 %weight_gradients.11 = bf16[2,2,8,64,512]{4,3,2,1,0:T(8,128)(2,1)} custom-call(s32[1]{0:T(128)} %bitcast.15.half, bf16[8,2,64,1024]{3,2,1,0:T(8,128)(2,1)} %get-tuple-element.66.refs_0_, bf16[8,2,64,1024]{3,2,1,0:T(8,128)(2,1)} %get-tuple-element.65.refs_0_.refs_1_, bf16[1024,1024]{1,0:T(8,128)(2,1)} %get-tuple-element.67.refs_2_, ...), custom_call_target="tpu_custom_call" | custom-call | flops 2147483648 | bytes 12582912 | tf_op jit(solution)/shard_map/weight_gradients/pallas_call | solution.py:457
  211.2 1.7 fusion.67
  214.4 21.0 %attention_backward.1 = (bf16[1024,1024]{1,0:T(8,128)(2,1)}, bf16[1024,1024]{1,0:T(8,128)(2,1)}, bf16[1024,1024]{1,0:T(8,128)(2,1)}) custom-call(s32[17]{0:T(128)} %concatenate.18.info, f32[8]{0:T(128)} %slopes.11, bf16[1024,1024]{1,0:T(8,128)(2,1)} %get-tuple-element.48.qpre.refs_23_, bf16[1024,1024]{1,0:T(8,128)(2,1)} %get-tuple-element.44.kpre, ...), custom_call_target="tpu_custom_call" | custom-call | flops 4831838208 | bytes 18874368 | tf_op jit(solution)/shard_map/attention_backward/pallas_call | solution.py:520
  236.4 1.5 collective-permute-start.35
  237.9 6.9 %weight_gradients.8 = bf16[2,3,8,64,512]{4,3,2,1,0:T(8,128)(2,1)} custom-call(s32[1]{0:T(128)S(6)} %sub.64.half, bf16[8,2,64,1024]{3,2,1,0:T(8,128)(2,1)} %get-tuple-element.65.refs_0_.refs_1_, bf16[1024,1024]{1,0:T(8,128)(2,1)} %get-tuple-element.60.refs_0_.refs_1_, bf16[1024,1024]{1,0:T(8,128)(2,1)} %get-tuple-element.61.refs_1_.refs_2_, ...), custom_call_target="tpu_custom_call" | custom-call | flops 3221225472 | bytes 11534336 | tf_op jit(solution)/shard_map/weight_gradients/pallas_call | solution.py:457
  245.6 5.6 %collective-permute-done.35 = bf16[2,2,2,64,512]{4,3,1,2,0:T(8,128)(2,1)S(1)} collective-permute-done((bf16[2,2,2,64,512]{4,3,1,2,0:T(8,128)(2,1)}, bf16[2,2,2,64,512]{4,3,1,2,0:T(8,128)(2,1)S(1)}, u32[]{:S(2)}, u32[]{:S(2)}) %collective-permute-start.35) | collective-permute-done | bytes 524320 | tf_op jit(solution)/shard_map/ppermute | solution.py:564
  251.3 1.6 collective-permute-start.36
  252.9 9.7 %weight_gradients.12 = bf16[2,3,8,64,768]{4,3,2,1,0:T(8,128)(2,1)} custom-call(s32[1]{0:T(128)S(6)} %sub.64.half, bf16[8,2,64,1024]{3,2,1,0:T(8,128)(2,1)} %get-tuple-element.68.refs_0_, bf16[8,2,64,1024]{3,2,1,0:T(8,128)(2,1)} %get-tuple-element.69.refs_1_, bf16[2,1024,768]{2,1,0:T(8,128)(2,1)} %get-tuple-element.70.refs_2_, ...), custom_call_target="tpu_custom_call" | custom-call | flops 4831838208 | bytes 18350080 | tf_op jit(solution)/shard_map/weight_gradients/pallas_call | solution.py:457
  265.8 2.6 collective-permute-start.40
  268.4 3.9 collective-permute-done.39
  272.3 1.5 collective-permute-start.41
  273.8 16.4 %input_gradient.1 = bf16[1024,1024]{1,0:T(8,128)(2,1)} custom-call(bf16[1024,1024]{1,0:T(8,128)(2,1)} %get-tuple-element.60.refs_0_.refs_1_, bf16[1024,1024]{1,0:T(8,128)(2,1)} %get-tuple-element.61.refs_1_.refs_2_, bf16[1024,1024]{1,0:T(8,128)(2,1)} %get-tuple-element.62.refs_2_.refs_3_, bf16[1024,1024]{1,0:T(8,128)(2,1)} %get-tuple-element.63.refs_3_, ...), custom_call_target="tpu_custom_call" | custom-call | flops 8589934592 | bytes 25165824 | tf_op jit(solution)/shard_map/input_gradient/pallas_call | solution.py:548
  291.1 1.6 copy-done
  292.7 7.5 %weight_gradients.9 = bf16[2,3,8,64,512]{4,3,2,1,0:T(8,128)(2,1)} custom-call(s32[1]{0:T(128)} %bitcast.15.half, bf16[8,2,64,1024]{3,2,1,0:T(8,128)(2,1)} %get-tuple-element.65.refs_0_.refs_1_, bf16[1024,1024]{1,0:T(8,128)(2,1)} %get-tuple-element.60.refs_0_.refs_1_, bf16[1024,1024]{1,0:T(8,128)(2,1)} %get-tuple-element.61.refs_1_.refs_2_, ...), custom_call_target="tpu_custom_call" | custom-call | flops 3221225472 | bytes 14680064 | tf_op jit(solution)/shard_map/weight_gradients/pallas_call | solution.py:457
  300.2 2.1 fusion.66
  303.2 1.9 collective-permute-start.27
  305.1 9.9 %weight_gradients.15 = bf16[2,3,8,64,640]{4,3,2,1,0:T(8,128)(2,1)} custom-call(s32[1]{0:T(128)} %bitcast.15.half, bf16[8,2,64,1024]{3,2,1,0:T(8,128)(2,1)} %get-tuple-element.68.refs_0_, bf16[8,2,64,1024]{3,2,1,0:T(8,128)(2,1)} %get-tuple-element.69.refs_1_, bf16[2,1024,640]{2,1,0:T(8,128)(2,1)} %get-tuple-element.73.refs_2_, ...), custom_call_target="tpu_custom_call" | custom-call | flops 4026531840 | bytes 19922944 | tf_op jit(solution)/shard_map/weight_gradients/pallas_call | solution.py:457
  315.0 2.6 fusion.65
  318.8 1.5 collective-permute-start.53
  322.4 1.4 fusion.4
  324.6 2.5 collective-permute-start.30
  327.1 1.4 fusion.5
  329.6 10.6 %weight_gradients.13 = bf16[2,3,8,64,768]{4,3,2,1,0:T(8,128)(2,1)} custom-call(s32[1]{0:T(128)} %bitcast.15.half, bf16[8,2,64,1024]{3,2,1,0:T(8,128)(2,1)} %get-tuple-element.68.refs_0_, bf16[8,2,64,1024]{3,2,1,0:T(8,128)(2,1)} %get-tuple-element.69.refs_1_, bf16[2,1024,768]{2,1,0:T(8,128)(2,1)} %get-tuple-element.70.refs_2_, ...), custom_call_target="tpu_custom_call" | custom-call | flops 4831838208 | bytes 23068672 | tf_op jit(solution)/shard_map/weight_gradients/pallas_call | solution.py:457
  340.2 2.7 fusion.64
  343.2 1.8 collective-permute-start.45
  345.3 7.4 %collective-permute-done.30 = bf16[3,2,64,512]{3,2,0,1:T(8,128)(2,1)} collective-permute-done((bf16[3,2,64,512]{3,2,0,1:T(8,128)(2,1)}, bf16[3,2,64,512]{3,2,0,1:T(8,128)(2,1)}, u32[]{:S(2)}, u32[]{:S(2)}) %collective-permute-start.30) | collective-permute-done | bytes 393248 | tf_op jit(solution)/shard_map/ppermute | solution.py:564
  354.8 3.3 collective-permute-start.31
  358.2 1.5 fusion.2
  359.7 1.6 collective-permute-start.33
  361.3 2.7 collective-permute-done.31
  365.6 5.4 %collective-permute-done.32 = bf16[3,64,512]{2,1,0:T(8,128)(2,1)S(1)} collective-permute-done((bf16[3,64,512]{2,1,0:T(8,128)(2,1)S(1)}, bf16[3,64,512]{2,1,0:T(8,128)(2,1)S(1)}, u32[]{:S(2)}, u32[]{:S(2)}) %collective-permute-start.32) | collective-permute-done | bytes 196640 | tf_op jit(solution)/shard_map/ppermute | solution.py:564
  371.0 1.9 collective-permute-start.52
  373.0 2.2 collective-permute-done.33
  375.3 13.4 %collective-permute-done.54 = bf16[3,2,64,640]{3,2,0,1:T(8,128)(2,1)S(1)} collective-permute-done((bf16[3,2,64,640]{3,2,0,1:T(8,128)(2,1)S(1)}, bf16[3,2,64,640]{3,2,0,1:T(8,128)(2,1)S(1)}, u32[]{:S(2)}, u32[]{:S(2)}) %collective-permute-start.54) | collective-permute-done | bytes 491552 | tf_op jit(solution)/shard_map/ppermute | solution.py:564
  391.1 2.1 collective-permute-start.44
  393.6 3.3 collective-permute-start.55
  397.0 1.5 collective-permute-start.57
  398.5 3.0 collective-permute-done.46
  401.6 2.6 collective-permute-done.44
  404.7 3.3 collective-permute-start.47
  408.1 1.5 collective-permute-start.49
  410.3 1.4 collective-permute-done.56
  411.8 20.4 %collective-permute-done.57 = bf16[3,64,640]{2,1,0:T(8,128)(2,1)S(1)} collective-permute-done((bf16[3,64,640]{2,1,0:T(8,128)(2,1)S(1)}, bf16[3,64,640]{2,1,0:T(8,128)(2,1)S(1)}, u32[]{:S(2)}, u32[]{:S(2)}) %collective-permute-start.57) | collective-permute-done | bytes 245792 | tf_op jit(solution)/shard_map/ppermute | solution.py:564
  432.4 4.6 %collective-permute-done.48 = bf16[3,64,768]{2,1,0:T(8,128)(2,1)S(1)} collective-permute-done((bf16[3,64,768]{2,1,0:T(8,128)(2,1)S(1)}, bf16[3,64,768]{2,1,0:T(8,128)(2,1)S(1)}, u32[]{:S(2)}, u32[]{:S(2)}) %collective-permute-start.48) | collective-permute-done | bytes 294944 | tf_op jit(solution)/shard_map/ppermute | solution.py:564
  437.1 5.7 %collective-permute-done.49 = bf16[3,64,768]{2,1,0:T(8,128)(2,1)S(1)} collective-permute-done((bf16[3,64,768]{2,1,0:T(8,128)(2,1)S(1)}, bf16[3,64,768]{2,1,0:T(8,128)(2,1)S(1)}, u32[]{:S(2)}, u32[]{:S(2)}) %collective-permute-start.49) | collective-permute-done | bytes 294944 | tf_op jit(solution)/shard_map/ppermute | solution.py:564
  (198 shorter events, 46.6 us)
Async XLA Ops:
  1.7 43.2 %collective-permute-start.13 = (bf16[256,768]{1,0:T(8,128)(2,1)S(1)}, bf16[256,768]{1,0:T(8,128)(2,1)S(1)}, u32[]{:S(2)}, u32[]{:S(2)}) collective-permute-start(bf16[256,768]{1,0:T(8,128)(2,1)S(1)} %constant_dynamic-slice_fusion.18), channel_id=1, source_target_pairs={{0,1},{1,0},{2,3},{3,2},{4,5},{5,4},{6,7},{7,6},{8,9},{9,8},{10,11... | collective-permute-start | bytes 1179656 | tf_op jit(solution)/shard_map/ppermute | solution.py:564
  3.3 42.1 %collective-permute-start.17 = (bf16[256,768]{1,0:T(8,128)(2,1)S(1)}, bf16[256,768]{1,0:T(8,128)(2,1)S(1)}, u32[]{:S(2)}, u32[]{:S(2)}) collective-permute-start(bf16[256,768]{1,0:T(8,128)(2,1)S(1)} %constant_dynamic-slice_fusion.17), channel_id=1, source_target_pairs={{0,1},{1,0},{2,3},{3,2},{4,5},{5,4},{6,7},{7,6},{8,9},{9,8},{10,11... | collective-permute-start | bytes 1179656 | tf_op jit(solution)/shard_map/ppermute | solution.py:564
  5.9 23.3 %collective-permute-start.9 = (bf16[160,1024]{1,0:T(8,128)(2,1)S(1)}, bf16[160,1024]{1,0:T(8,128)(2,1)S(1)}, u32[]{:S(2)}, u32[]{:S(2)}) collective-permute-start(bf16[160,1024]{1,0:T(8,128)(2,1)S(1)} %constant_dynamic-slice_fusion.19), channel_id=1, source_target_pairs={{0,1},{1,0},{2,3},{3,2},{4,5},{5,4},{6,7},{7,6},{8,9},{9,8},{10,11... | collective-permute-start | bytes 983048 | tf_op jit(solution)/shard_map/ppermute | solution.py:564
  7.5 28.9 %collective-permute-start.1 = (bf16[256,640]{1,0:T(8,128)(2,1)S(1)}, bf16[256,640]{1,0:T(8,128)(2,1)}, u32[]{:S(2)}, u32[]{:S(2)}) collective-permute-start(bf16[256,640]{1,0:T(8,128)(2,1)S(1)} %constant_dynamic-slice_fusion.21), channel_id=1, source_target_pairs={{0,1},{1,0},{2,3},{3,2},{4,5},{5,4},{6,7},{7,6},{8,9},{9,8},{10,11... | collective-permute-start | bytes 983048 | tf_op jit(solution)/shard_map/ppermute | solution.py:564
  10.0 33.3 %collective-permute-start.5 = (bf16[256,640]{1,0:T(8,128)(2,1)S(1)}, bf16[256,640]{1,0:T(8,128)(2,1)}, u32[]{:S(2)}, u32[]{:S(2)}) collective-permute-start(bf16[256,640]{1,0:T(8,128)(2,1)S(1)} %constant_dynamic-slice_fusion.20), channel_id=1, source_target_pairs={{0,1},{1,0},{2,3},{3,2},{4,5},{5,4},{6,7},{7,6},{8,9},{9,8},{10,11... | collective-permute-start | bytes 983048 | tf_op jit(solution)/shard_map/ppermute | solution.py:564
  29.2 32.6 %collective-permute-start = (bf16[8,128,256]{2,1,0:T(8,128)(2,1)}, bf16[8,128,256]{2,1,0:T(8,128)(2,1)S(1)}, u32[]{:S(2)}, u32[]{:S(2)}) collective-permute-start(bf16[8,128,256]{2,1,0:T(8,128)(2,1)} %get-tuple-element.49), channel_id=1, source_target_pairs={{0,1},{1,0},{2,3},{3,2},{4,5},{5,4},{6,7},{7,6},{8,9},{9,8},{10,11... | collective-permute-start | bytes 1572872 | tf_op jit(solution)/shard_map/ppermute | solution.py:564
  36.3 25.4 %collective-permute-start.21 = (bf16[192,1024]{1,0:T(8,128)(2,1)S(1)}, bf16[192,1024]{1,0:T(8,128)(2,1)S(1)}, u32[]{:S(2)}, u32[]{:S(2)}) collective-permute-start(bf16[192,1024]{1,0:T(8,128)(2,1)S(1)} %constant_dynamic-slice_fusion.16), channel_id=1, source_target_pairs={{0,1},{1,0},{2,3},{3,2},{4,5},{5,4},{6,7},{7,6},{8,9},{9,8},{10,11... | collective-permute-start | bytes 1179656 | tf_op jit(solution)/shard_map/ppermute | solution.py:564
  43.4 20.0 %collective-permute-start.10 = (bf16[160,1024]{1,0:T(8,128)(2,1)}, bf16[160,1024]{1,0:T(8,128)(2,1)S(1)}, u32[]{:S(2)}, u32[]{:S(2)}) collective-permute-start(bf16[160,1024]{1,0:T(8,128)(2,1)} %copy-done.17), channel_id=1, source_target_pairs={{0,4},{2,6},{4,0},{6,2},{8,12},{10,14},{12,8},{14,10},{16,20},{18,... | collective-permute-start | bytes 983048 | tf_op jit(solution)/shard_map/ppermute | solution.py:564
  44.9 35.9 %copy-start.5 = (bf16[256,768]{1,0:T(8,128)(2,1)}, bf16[256,768]{1,0:T(8,128)(2,1)S(1)}, u32[]{:S(2)}) copy-start(bf16[256,768]{1,0:T(8,128)(2,1)S(1)} %collective-permute-done.13.refs_3_) | copy-start | bytes 1179652
  44.9 19.2 %collective-permute-start.2 = (bf16[256,640]{1,0:T(8,128)(2,1)}, bf16[256,640]{1,0:T(8,128)(2,1)}, u32[]{:S(2)}, u32[]{:S(2)}) collective-permute-start(bf16[256,640]{1,0:T(8,128)(2,1)} %collective-permute-done.1.refs_3_), channel_id=1, source_target_pairs={{0,4},{2,6},{4,0},{6,2},{8,12},{10,14},{12,8},{14,10},{16,20},{18,... | collective-permute-start | bytes 983048 | tf_op jit(solution)/shard_map/ppermute | solution.py:564
  45.4 35.3 %copy-start.6 = (bf16[256,768]{1,0:T(8,128)(2,1)}, bf16[256,768]{1,0:T(8,128)(2,1)S(1)}, u32[]{:S(2)}) copy-start(bf16[256,768]{1,0:T(8,128)(2,1)S(1)} %collective-permute-done.17.refs_8_) | copy-start | bytes 1179652
  45.4 19.9 %collective-permute-start.6 = (bf16[256,640]{1,0:T(8,128)(2,1)}, bf16[256,640]{1,0:T(8,128)(2,1)}, u32[]{:S(2)}, u32[]{:S(2)}) collective-permute-start(bf16[256,640]{1,0:T(8,128)(2,1)} %collective-permute-done.5.refs_8_), channel_id=1, source_target_pairs={{0,4},{2,6},{4,0},{6,2},{8,12},{10,14},{12,8},{14,10},{16,20},{18,... | collective-permute-start | bytes 983048 | tf_op jit(solution)/shard_map/ppermute | solution.py:564
  61.8 19.1 %copy-start.7 = (bf16[192,1024]{1,0:T(8,128)(2,1)}, bf16[192,1024]{1,0:T(8,128)(2,1)S(1)}, u32[]{:S(2)}) copy-start(bf16[192,1024]{1,0:T(8,128)(2,1)S(1)} %collective-permute-done.21.refs_13_) | copy-start | bytes 1179652
  61.8 19.0 %collective-permute-start.11 = (bf16[160,1024]{1,0:T(8,128)(2,1)}, bf16[160,1024]{1,0:T(8,128)(2,1)S(1)}, u32[]{:S(2)}, u32[]{:S(2)}) collective-permute-start(bf16[160,1024]{1,0:T(8,128)(2,1)} %copy-done.17), channel_id=1, source_target_pairs={{0,2},{2,0},{4,6},{6,4},{8,10},{10,8},{12,14},{14,12},{16,18},{18,... | collective-permute-start | bytes 983048 | tf_op jit(solution)/shard_map/ppermute | solution.py:564
  61.8 19.1 %collective-permute-start.14 = (bf16[256,768]{1,0:T(8,128)(2,1)S(1)}, bf16[256,768]{1,0:T(8,128)(2,1)S(1)}, u32[]{:S(2)}, u32[]{:S(2)}) collective-permute-start(bf16[256,768]{1,0:T(8,128)(2,1)S(1)} %collective-permute-done.13.refs_3_), channel_id=1, source_target_pairs={{0,4},{2,6},{4,0},{6,2},{8,12},{10,14},{12,8},{14,10},{16,20},{18,... | collective-permute-start | bytes 1179656 | tf_op jit(solution)/shard_map/ppermute | solution.py:564
  63.4 27.0 %collective-permute-start.15 = (bf16[256,768]{1,0:T(8,128)(2,1)S(1)}, bf16[256,768]{1,0:T(8,128)(2,1)S(1)}, u32[]{:S(2)}, u32[]{:S(2)}) collective-permute-start(bf16[256,768]{1,0:T(8,128)(2,1)S(1)} %collective-permute-done.13.refs_3_), channel_id=1, source_target_pairs={{0,2},{2,0},{4,6},{6,4},{8,10},{10,8},{12,14},{14,12},{16,18},{18,... | collective-permute-start | bytes 1179656 | tf_op jit(solution)/shard_map/ppermute | solution.py:564
  64.1 18.1 %collective-permute-start.18 = (bf16[256,768]{1,0:T(8,128)(2,1)S(1)}, bf16[256,768]{1,0:T(8,128)(2,1)S(1)}, u32[]{:S(2)}, u32[]{:S(2)}) collective-permute-start(bf16[256,768]{1,0:T(8,128)(2,1)S(1)} %collective-permute-done.17.refs_8_), channel_id=1, source_target_pairs={{0,4},{2,6},{4,0},{6,2},{8,12},{10,14},{12,8},{14,10},{16,20},{18,... | collective-permute-start | bytes 1179656 | tf_op jit(solution)/shard_map/ppermute | solution.py:564
  65.3 25.1 %collective-permute-start.22 = (bf16[192,1024]{1,0:T(8,128)(2,1)S(1)}, bf16[192,1024]{1,0:T(8,128)(2,1)S(1)}, u32[]{:S(2)}, u32[]{:S(2)}) collective-permute-start(bf16[192,1024]{1,0:T(8,128)(2,1)S(1)} %collective-permute-done.21.refs_13_), channel_id=1, source_target_pairs={{0,4},{2,6},{4,0},{6,2},{8,12},{10,14},{12,8},{14,10},{16,20},{18,... | collective-permute-start | bytes 1179656 | tf_op jit(solution)/shard_map/ppermute | solution.py:564
  80.8 25.0 %copy-start.20 = (bf16[160,1024]{1,0:T(8,128)(2,1)}, bf16[160,1024]{1,0:T(8,128)(2,1)S(1)}, u32[]{:S(2)}) copy-start(bf16[160,1024]{1,0:T(8,128)(2,1)S(1)} %collective-permute-done.11.refs_15_) | copy-start | bytes 983044
  80.8 25.1 %collective-permute-start.19 = (bf16[256,768]{1,0:T(8,128)(2,1)S(1)}, bf16[256,768]{1,0:T(8,128)(2,1)S(1)}, u32[]{:S(2)}, u32[]{:S(2)}) collective-permute-start(bf16[256,768]{1,0:T(8,128)(2,1)S(1)} %collective-permute-done.17.refs_8_), channel_id=1, source_target_pairs={{0,2},{2,0},{4,6},{6,4},{8,10},{10,8},{12,14},{14,12},{16,18},{18,... | collective-permute-start | bytes 1179656 | tf_op jit(solution)/shard_map/ppermute | solution.py:564
  80.9 24.9 %copy-start.8 = (bf16[256,768]{1,0:T(8,128)(2,1)}, bf16[256,768]{1,0:T(8,128)(2,1)S(1)}, u32[]{:S(2)}) copy-start(bf16[256,768]{1,0:T(8,128)(2,1)S(1)} %collective-permute-done.14.refs_4_) | copy-start | bytes 1179652
  80.9 25.1 %collective-permute-start.23 = (bf16[192,1024]{1,0:T(8,128)(2,1)S(1)}, bf16[192,1024]{1,0:T(8,128)(2,1)S(1)}, u32[]{:S(2)}, u32[]{:S(2)}) collective-permute-start(bf16[192,1024]{1,0:T(8,128)(2,1)S(1)} %collective-permute-done.21.refs_13_), channel_id=1, source_target_pairs={{0,2},{2,0},{4,6},{6,4},{8,10},{10,8},{12,14},{14,12},{16,18},{18,... | collective-permute-start | bytes 1179656 | tf_op jit(solution)/shard_map/ppermute | solution.py:564
  82.2 23.6 %copy-start.10 = (bf16[256,768]{1,0:T(8,128)(2,1)}, bf16[256,768]{1,0:T(8,128)(2,1)S(1)}, u32[]{:S(2)}) copy-start(bf16[256,768]{1,0:T(8,128)(2,1)S(1)} %collective-permute-done.18.refs_9_) | copy-start | bytes 1179652
  82.2 24.2 %collective-permute-start.16 = (bf16[256,768]{1,0:T(8,128)(2,1)S(1)}, bf16[256,768]{1,0:T(8,128)(2,1)S(1)}, u32[]{:S(2)}, u32[]{:S(2)}) collective-permute-start(bf16[256,768]{1,0:T(8,128)(2,1)S(1)} %collective-permute-done.14.refs_4_), channel_id=1, source_target_pairs={{0,2},{2,0},{4,6},{6,4},{8,10},{10,8},{12,14},{14,12},{16,18},{18,... | collective-permute-start | bytes 1179656 | tf_op jit(solution)/shard_map/ppermute | solution.py:564
  90.3 16.3 %collective-permute-start.20 = (bf16[256,768]{1,0:T(8,128)(2,1)S(1)}, bf16[256,768]{1,0:T(8,128)(2,1)S(1)}, u32[]{:S(2)}, u32[]{:S(2)}) collective-permute-start(bf16[256,768]{1,0:T(8,128)(2,1)S(1)} %collective-permute-done.18.refs_9_), channel_id=1, source_target_pairs={{0,2},{2,0},{4,6},{6,4},{8,10},{10,8},{12,14},{14,12},{16,18},{18,... | collective-permute-start | bytes 1179656 | tf_op jit(solution)/shard_map/ppermute | solution.py:564
  90.4 16.7 %collective-permute-start.24 = (bf16[192,1024]{1,0:T(8,128)(2,1)S(1)}, bf16[192,1024]{1,0:T(8,128)(2,1)S(1)}, u32[]{:S(2)}, u32[]{:S(2)}) collective-permute-start(bf16[192,1024]{1,0:T(8,128)(2,1)S(1)} %collective-permute-done.22.refs_14_), channel_id=1, source_target_pairs={{0,2},{2,0},{4,6},{6,4},{8,10},{10,8},{12,14},{14,12},{16,18},{18,... | collective-permute-start | bytes 1179656 | tf_op jit(solution)/shard_map/ppermute | solution.py:564
  105.8 35.9 %collective-permute-start.3 = (bf16[256,640]{1,0:T(8,128)(2,1)}, bf16[256,640]{1,0:T(8,128)(2,1)S(1)}, u32[]{:S(2)}, u32[]{:S(2)}) collective-permute-start(bf16[256,640]{1,0:T(8,128)(2,1)} %collective-permute-done.1.refs_3_), channel_id=1, source_target_pairs={{0,2},{2,0},{4,6},{6,4},{8,10},{10,8},{12,14},{14,12},{16,18},{18,... | collective-permute-start | bytes 983048 | tf_op jit(solution)/shard_map/ppermute | solution.py:564
  106.0 35.7 %collective-permute-start.7 = (bf16[256,640]{1,0:T(8,128)(2,1)}, bf16[256,640]{1,0:T(8,128)(2,1)S(1)}, u32[]{:S(2)}, u32[]{:S(2)}) collective-permute-start(bf16[256,640]{1,0:T(8,128)(2,1)} %collective-permute-done.5.refs_8_), channel_id=1, source_target_pairs={{0,2},{2,0},{4,6},{6,4},{8,10},{10,8},{12,14},{14,12},{16,18},{18,... | collective-permute-start | bytes 983048 | tf_op jit(solution)/shard_map/ppermute | solution.py:564
  106.4 35.3 %collective-permute-start.12 = (bf16[160,1024]{1,0:T(8,128)(2,1)S(1)}, bf16[160,1024]{1,0:T(8,128)(2,1)S(1)}, u32[]{:S(2)}, u32[]{:S(2)}) collective-permute-start(bf16[160,1024]{1,0:T(8,128)(2,1)S(1)} %copy-done.19), channel_id=1, source_target_pairs={{0,2},{2,0},{4,6},{6,4},{8,10},{10,8},{12,14},{14,12},{16,18},{18,... | collective-permute-start | bytes 983048 | tf_op jit(solution)/shard_map/ppermute | solution.py:564
  106.6 35.2 %collective-permute-start.4 = (bf16[256,640]{1,0:T(8,128)(2,1)}, bf16[256,640]{1,0:T(8,128)(2,1)S(1)}, u32[]{:S(2)}, u32[]{:S(2)}) collective-permute-start(bf16[256,640]{1,0:T(8,128)(2,1)} %collective-permute-done.2.refs_4_), channel_id=1, source_target_pairs={{0,2},{2,0},{4,6},{6,4},{8,10},{10,8},{12,14},{14,12},{16,18},{18,... | collective-permute-start | bytes 983048 | tf_op jit(solution)/shard_map/ppermute | solution.py:564
  107.0 34.8 %collective-permute-start.8 = (bf16[256,640]{1,0:T(8,128)(2,1)}, bf16[256,640]{1,0:T(8,128)(2,1)S(1)}, u32[]{:S(2)}, u32[]{:S(2)}) collective-permute-start(bf16[256,640]{1,0:T(8,128)(2,1)} %collective-permute-done.6.refs_9_), channel_id=1, source_target_pairs={{0,2},{2,0},{4,6},{6,4},{8,10},{10,8},{12,14},{14,12},{16,18},{18,... | collective-permute-start | bytes 983048 | tf_op jit(solution)/shard_map/ppermute | solution.py:564
  188.7 15.2 %collective-permute-start.34 = (bf16[2,2,8,64,512]{4,3,2,1,0:T(8,128)(2,1)}, bf16[2,2,8,64,512]{4,3,2,1,0:T(8,128)(2,1)S(1)}, u32[]{:S(2)}, u32[]{:S(2)}) collective-permute-start(bf16[2,2,8,64,512]{4,3,2,1,0:T(8,128)(2,1)} %weight_gradients.10), channel_id=1, source_target_pairs={{0,2},{2,0},{4,6},{6,4},{8,10},{10,8},{12,14},{14,12},{16,18},{18,... | collective-permute-start | bytes 6291464 | tf_op jit(solution)/shard_map/ppermute | solution.py:564
  188.8 14.2 %collective-permute-start.25 = (bf16[8,128,256]{2,1,0:T(8,128)(2,1)S(1)}, bf16[8,128,256]{2,1,0:T(8,128)(2,1)S(1)}, u32[]{:S(2)}, u32[]{:S(2)}) collective-permute-start(bf16[8,128,256]{2,1,0:T(8,128)(2,1)S(1)} %copy-done.4), channel_id=1, source_target_pairs={{0,1},{1,0},{2,3},{3,2},{4,5},{5,4},{6,7},{7,6},{8,9},{9,8},{10,11... | collective-permute-start | bytes 1572872 | tf_op jit(solution)/shard_map/ppermute | solution.py:564
  198.6 106.5 %collective-permute-start.50 = (bf16[2,3,8,64,640]{4,3,2,1,0:T(8,128)(2,1)}, bf16[2,3,8,64,640]{4,3,2,1,0:T(8,128)(2,1)}, u32[]{:S(2)}, u32[]{:S(2)}) collective-permute-start(bf16[2,3,8,64,640]{4,3,2,1,0:T(8,128)(2,1)} %weight_gradients.14), channel_id=1, source_target_pairs={{0,2},{2,0},{4,6},{6,4},{8,10},{10,8},{12,14},{14,12},{16,18},{18,... | collective-permute-start | bytes 11796488 | tf_op jit(solution)/shard_map/ppermute | solution.py:564
  213.9 30.9 %collective-permute-start.37 = (bf16[2,2,2,64,512]{4,3,0,1,2:T(8,128)(2,1)}, bf16[2,2,2,64,512]{4,3,0,1,2:T(8,128)(2,1)S(1)}, u32[]{:S(2)}, u32[]{:S(2)}) collective-permute-start(bf16[2,2,2,64,512]{4,3,0,1,2:T(8,128)(2,1)} %bitcast.192), channel_id=1, source_target_pairs={{0,1},{1,0},{2,3},{3,2},{4,5},{5,4},{6,7},{7,6},{8,9},{9,8},{10,11... | collective-permute-start | bytes 1572872 | tf_op jit(solution)/shard_map/ppermute | solution.py:564
  236.4 14.8 %collective-permute-start.35 = (bf16[2,2,2,64,512]{4,3,1,2,0:T(8,128)(2,1)}, bf16[2,2,2,64,512]{4,3,1,2,0:T(8,128)(2,1)S(1)}, u32[]{:S(2)}, u32[]{:S(2)}) collective-permute-start(bf16[2,2,2,64,512]{4,3,1,2,0:T(8,128)(2,1)} %bitcast.193), channel_id=1, source_target_pairs={{0,4},{2,6},{4,0},{6,2},{8,12},{10,14},{12,8},{14,10},{16,20},{18,... | collective-permute-start | bytes 1572872 | tf_op jit(solution)/shard_map/ppermute | solution.py:564
  244.8 46.3 %collective-permute-start.26 = (bf16[2,3,8,64,512]{4,3,2,1,0:T(8,128)(2,1)}, bf16[2,3,8,64,512]{4,3,2,1,0:T(8,128)(2,1)S(1)}, u32[]{:S(2)}, u32[]{:S(2)}) collective-permute-start(bf16[2,3,8,64,512]{4,3,2,1,0:T(8,128)(2,1)} %weight_gradients.8), channel_id=1, source_target_pairs={{0,2},{2,0},{4,6},{6,4},{8,10},{10,8},{12,14},{14,12},{16,18},{18,... | collective-permute-start | bytes 9437192 | tf_op jit(solution)/shard_map/ppermute | solution.py:564
  245.0 17.6 %collective-permute-start.38 = (bf16[2,2,64,512]{3,2,0,1:T(8,128)(2,1)S(1)}, bf16[2,2,64,512]{3,2,0,1:T(8,128)(2,1)}, u32[]{:S(2)}, u32[]{:S(2)}) collective-permute-start(bf16[2,2,64,512]{3,2,0,1:T(8,128)(2,1)S(1)} %dynamic-slice_bitcast_fusion.6), channel_id=1, source_target_pairs={{0,4},{2,6},{4,0},{6,2},{8,12},{10,14},{12,8},{14,10},{16,20},{18,... | collective-permute-start | bytes 786440 | tf_op jit(solution)/shard_map/ppermute | solution.py:564
  251.3 12.3 %collective-permute-start.36 = (bf16[2,2,64,512]{3,2,0,1:T(8,128)(2,1)S(1)}, bf16[2,2,64,512]{3,2,0,1:T(8,128)(2,1)S(1)}, u32[]{:S(2)}, u32[]{:S(2)}) collective-permute-start(bf16[2,2,64,512]{3,2,0,1:T(8,128)(2,1)S(1)} %dynamic-slice_bitcast_fusion.7), channel_id=1, source_target_pairs={{0,1},{1,0},{2,3},{3,2},{4,5},{5,4},{6,7},{7,6},{8,9},{9,8},{10,11... | collective-permute-start | bytes 786440 | tf_op jit(solution)/shard_map/ppermute | solution.py:564
  262.6 67.0 %collective-permute-start.42 = (bf16[2,3,8,64,768]{4,3,2,1,0:T(8,128)(2,1)}, bf16[2,3,8,64,768]{4,3,2,1,0:T(8,128)(2,1)}, u32[]{:S(2)}, u32[]{:S(2)}) collective-permute-start(bf16[2,3,8,64,768]{4,3,2,1,0:T(8,128)(2,1)} %weight_gradients.12), channel_id=1, source_target_pairs={{0,2},{2,0},{4,6},{6,4},{8,10},{10,8},{12,14},{14,12},{16,18},{18,... | collective-permute-start | bytes 14155784 | tf_op jit(solution)/shard_map/ppermute | solution.py:564
  265.3 7.0 %collective-permute-start.39 = (bf16[2,64,512]{2,1,0:T(8,128)(2,1)}, bf16[2,64,512]{2,1,0:T(8,128)(2,1)S(1)}, u32[]{:S(2)}, u32[]{:S(2)}) collective-permute-start(bf16[2,64,512]{2,1,0:T(8,128)(2,1)} %get-tuple-element.114), channel_id=1, source_target_pairs={{0,8},{2,10},{4,12},{6,14},{8,0},{10,2},{12,4},{14,6},{16,24},{18,... | collective-permute-start | bytes 393224 | tf_op jit(solution)/shard_map/ppermute | solution.py:564
  265.8 24.4 %collective-permute-start.40 = (bf16[2,64,512]{2,1,0:T(8,128)(2,1)}, bf16[2,64,512]{2,1,0:T(8,128)(2,1)S(1)}, u32[]{:S(2)}, u32[]{:S(2)}) collective-permute-start(bf16[2,64,512]{2,1,0:T(8,128)(2,1)} %get-tuple-element.115), channel_id=1, source_target_pairs={{0,16},{2,18},{4,20},{6,22},{8,24},{10,26},{12,28},{14,30},{16,0},... | collective-permute-start | bytes 393224 | tf_op jit(solution)/shard_map/ppermute | solution.py:564
  272.3 18.0 %collective-permute-start.41 = (bf16[2,64,512]{2,1,0:T(8,128)(2,1)}, bf16[2,64,512]{2,1,0:T(8,128)(2,1)S(1)}, u32[]{:S(2)}, u32[]{:S(2)}) collective-permute-start(bf16[2,64,512]{2,1,0:T(8,128)(2,1)} %get-tuple-element.116), channel_id=1, source_target_pairs={{0,24},{2,26},{4,28},{6,30},{8,16},{10,18},{12,20},{14,22},{16,8},... | collective-permute-start | bytes 393224 | tf_op jit(solution)/shard_map/ppermute | solution.py:564
  302.5 20.0 %collective-permute-start.29 = (bf16[3,2,2,64,512]{4,3,0,1,2:T(8,128)(2,1)S(1)}, bf16[3,2,2,64,512]{4,3,0,1,2:T(8,128)(2,1)}, u32[]{:S(2)}, u32[]{:S(2)}) collective-permute-start(bf16[3,2,2,64,512]{4,3,0,1,2:T(8,128)(2,1)S(1)} %bitcast.201), channel_id=1, source_target_pairs={{0,1},{1,0},{2,3},{3,2},{4,5},{5,4},{6,7},{7,6},{8,9},{9,8},{10,11... | collective-permute-start | bytes 2359304 | tf_op jit(solution)/shard_map/ppermute | solution.py:564
  303.2 23.9 %collective-permute-start.27 = (bf16[2,3,2,64,512]{4,3,1,2,0:T(8,128)(2,1)S(1)}, bf16[2,3,2,64,512]{4,3,1,2,0:T(8,128)(2,1)}, u32[]{:S(2)}, u32[]{:S(2)}) collective-permute-start(bf16[2,3,2,64,512]{4,3,1,2,0:T(8,128)(2,1)S(1)} %bitcast.200), channel_id=1, source_target_pairs={{0,4},{2,6},{4,0},{6,2},{8,12},{10,14},{12,8},{14,10},{16,20},{18,... | collective-permute-start | bytes 2359304 | tf_op jit(solution)/shard_map/ppermute | solution.py:564
  318.8 39.4 %collective-permute-start.53 = (bf16[3,2,2,64,640]{4,3,0,1,2:T(8,128)(2,1)}, bf16[3,2,2,64,640]{4,3,0,1,2:T(8,128)(2,1)}, u32[]{:S(2)}, u32[]{:S(2)}) collective-permute-start(bf16[3,2,2,64,640]{4,3,0,1,2:T(8,128)(2,1)} %bitcast.188), channel_id=1, source_target_pairs={{0,1},{1,0},{2,3},{3,2},{4,5},{5,4},{6,7},{7,6},{8,9},{9,8},{10,11... | collective-permute-start | bytes 2949128 | tf_op jit(solution)/shard_map/ppermute | solution.py:564
  321.6 38.1 %collective-permute-start.51 = (bf16[2,3,2,64,640]{4,3,1,2,0:T(8,128)(2,1)}, bf16[2,3,2,64,640]{4,3,1,2,0:T(8,128)(2,1)S(1)}, u32[]{:S(2)}, u32[]{:S(2)}) collective-permute-start(bf16[2,3,2,64,640]{4,3,1,2,0:T(8,128)(2,1)} %bitcast.189), channel_id=1, source_target_pairs={{0,4},{2,6},{4,0},{6,2},{8,12},{10,14},{12,8},{14,10},{16,20},{18,... | collective-permute-start | bytes 2949128 | tf_op jit(solution)/shard_map/ppermute | solution.py:564
  324.6 28.0 %collective-permute-start.30 = (bf16[3,2,64,512]{3,2,0,1:T(8,128)(2,1)}, bf16[3,2,64,512]{3,2,0,1:T(8,128)(2,1)}, u32[]{:S(2)}, u32[]{:S(2)}) collective-permute-start(bf16[3,2,64,512]{3,2,0,1:T(8,128)(2,1)} %dynamic-slice_bitcast_fusion.4), channel_id=1, source_target_pairs={{0,4},{2,6},{4,0},{6,2},{8,12},{10,14},{12,8},{14,10},{16,20},{18,... | collective-permute-start | bytes 1179656 | tf_op jit(solution)/shard_map/ppermute | solution.py:564
  329.3 25.2 %collective-permute-start.28 = (bf16[3,2,64,512]{3,2,0,1:T(8,128)(2,1)}, bf16[3,2,64,512]{3,2,0,1:T(8,128)(2,1)S(1)}, u32[]{:S(2)}, u32[]{:S(2)}) collective-permute-start(bf16[3,2,64,512]{3,2,0,1:T(8,128)(2,1)} %dynamic-slice_bitcast_fusion.5), channel_id=1, source_target_pairs={{0,1},{1,0},{2,3},{3,2},{4,5},{5,4},{6,7},{7,6},{8,9},{9,8},{10,11... | collective-permute-start | bytes 1179656 | tf_op jit(solution)/shard_map/ppermute | solution.py:564
  343.2 45.7 %collective-permute-start.45 = (bf16[3,2,2,64,768]{4,3,0,1,2:T(8,128)(2,1)S(1)}, bf16[3,2,2,64,768]{4,3,0,1,2:T(8,128)(2,1)S(1)}, u32[]{:S(2)}, u32[]{:S(2)}) collective-permute-start(bf16[3,2,2,64,768]{4,3,0,1,2:T(8,128)(2,1)S(1)} %bitcast.199), channel_id=1, source_target_pairs={{0,1},{1,0},{2,3},{3,2},{4,5},{5,4},{6,7},{7,6},{8,9},{9,8},{10,11... | collective-permute-start | bytes 3538952 | tf_op jit(solution)/shard_map/ppermute | solution.py:564
  352.6 38.0 %collective-permute-start.43 = (bf16[2,3,2,64,768]{4,3,1,2,0:T(8,128)(2,1)S(1)}, bf16[2,3,2,64,768]{4,3,1,2,0:T(8,128)(2,1)S(1)}, u32[]{:S(2)}, u32[]{:S(2)}) collective-permute-start(bf16[2,3,2,64,768]{4,3,1,2,0:T(8,128)(2,1)S(1)} %bitcast.198), channel_id=1, source_target_pairs={{0,4},{2,6},{4,0},{6,2},{8,12},{10,14},{12,8},{14,10},{16,20},{18,... | collective-permute-start | bytes 3538952 | tf_op jit(solution)/shard_map/ppermute | solution.py:564
  354.8 9.2 %collective-permute-start.31 = (bf16[3,64,512]{2,1,0:T(8,128)(2,1)S(1)}, bf16[3,64,512]{2,1,0:T(8,128)(2,1)S(1)}, u32[]{:S(2)}, u32[]{:S(2)}) collective-permute-start(bf16[3,64,512]{2,1,0:T(8,128)(2,1)S(1)} %get-tuple-element.111), channel_id=1, source_target_pairs={{0,8},{2,10},{4,12},{6,14},{8,0},{10,2},{12,4},{14,6},{16,24},{18,... | collective-permute-start | bytes 589832 | tf_op jit(solution)/shard_map/ppermute | solution.py:564
  358.2 12.9 %collective-permute-start.32 = (bf16[3,64,512]{2,1,0:T(8,128)(2,1)S(1)}, bf16[3,64,512]{2,1,0:T(8,128)(2,1)S(1)}, u32[]{:S(2)}, u32[]{:S(2)}) collective-permute-start(bf16[3,64,512]{2,1,0:T(8,128)(2,1)S(1)} %get-tuple-element.112), channel_id=1, source_target_pairs={{0,16},{2,18},{4,20},{6,22},{8,24},{10,26},{12,28},{14,30},{16,0},... | collective-permute-start | bytes 589832 | tf_op jit(solution)/shard_map/ppermute | solution.py:564
  359.7 15.5 %collective-permute-start.33 = (bf16[3,64,512]{2,1,0:T(8,128)(2,1)S(1)}, bf16[3,64,512]{2,1,0:T(8,128)(2,1)S(1)}, u32[]{:S(2)}, u32[]{:S(2)}) collective-permute-start(bf16[3,64,512]{2,1,0:T(8,128)(2,1)S(1)} %get-tuple-element.113), channel_id=1, source_target_pairs={{0,24},{2,26},{4,28},{6,30},{8,16},{10,18},{12,20},{14,22},{16,8},... | collective-permute-start | bytes 589832 | tf_op jit(solution)/shard_map/ppermute | solution.py:564
  364.0 24.8 %collective-permute-start.54 = (bf16[3,2,64,640]{3,2,0,1:T(8,128)(2,1)S(1)}, bf16[3,2,64,640]{3,2,0,1:T(8,128)(2,1)S(1)}, u32[]{:S(2)}, u32[]{:S(2)}) collective-permute-start(bf16[3,2,64,640]{3,2,0,1:T(8,128)(2,1)S(1)} %dynamic-slice_bitcast_fusion.2), channel_id=1, source_target_pairs={{0,4},{2,6},{4,0},{6,2},{8,12},{10,14},{12,8},{14,10},{16,20},{18,... | collective-permute-start | bytes 1474568 | tf_op jit(solution)/shard_map/ppermute | solution.py:564
  371.0 22.1 %collective-permute-start.52 = (bf16[3,2,64,640]{3,2,0,1:T(8,128)(2,1)S(1)}, bf16[3,2,64,640]{3,2,0,1:T(8,128)(2,1)S(1)}, u32[]{:S(2)}, u32[]{:S(2)}) collective-permute-start(bf16[3,2,64,640]{3,2,0,1:T(8,128)(2,1)S(1)} %dynamic-slice_bitcast_fusion.3), channel_id=1, source_target_pairs={{0,1},{1,0},{2,3},{3,2},{4,5},{5,4},{6,7},{7,6},{8,9},{9,8},{10,11... | collective-permute-start | bytes 1474568 | tf_op jit(solution)/shard_map/ppermute | solution.py:564
  389.3 12.1 %collective-permute-start.46 = (bf16[3,2,64,768]{3,2,0,1:T(8,128)(2,1)S(1)}, bf16[3,2,64,768]{3,2,0,1:T(8,128)(2,1)S(1)}, u32[]{:S(2)}, u32[]{:S(2)}) collective-permute-start(bf16[3,2,64,768]{3,2,0,1:T(8,128)(2,1)S(1)} %dynamic-slice_bitcast_fusion), channel_id=1, source_target_pairs={{0,4},{2,6},{4,0},{6,2},{8,12},{10,14},{12,8},{14,10},{16,20},{18,... | collective-permute-start | bytes 1769480 | tf_op jit(solution)/shard_map/ppermute | solution.py:564
  391.1 13.1 %collective-permute-start.44 = (bf16[3,2,64,768]{3,2,0,1:T(8,128)(2,1)S(1)}, bf16[3,2,64,768]{3,2,0,1:T(8,128)(2,1)S(1)}, u32[]{:S(2)}, u32[]{:S(2)}) collective-permute-start(bf16[3,2,64,768]{3,2,0,1:T(8,128)(2,1)S(1)} %dynamic-slice_bitcast_fusion.1), channel_id=1, source_target_pairs={{0,1},{1,0},{2,3},{3,2},{4,5},{5,4},{6,7},{7,6},{8,9},{9,8},{10,11... | collective-permute-start | bytes 1769480 | tf_op jit(solution)/shard_map/ppermute | solution.py:564
  393.6 14.4 %collective-permute-start.55 = (bf16[3,64,640]{2,1,0:T(8,128)(2,1)S(1)}, bf16[3,64,640]{2,1,0:T(8,128)(2,1)S(1)}, u32[]{:S(2)}, u32[]{:S(2)}) collective-permute-start(bf16[3,64,640]{2,1,0:T(8,128)(2,1)S(1)} %get-tuple-element.108), channel_id=1, source_target_pairs={{0,8},{2,10},{4,12},{6,14},{8,0},{10,2},{12,4},{14,6},{16,24},{18,... | collective-permute-start | bytes 737288 | tf_op jit(solution)/shard_map/ppermute | solution.py:564
  397.0 14.8 %collective-permute-start.56 = (bf16[3,64,640]{2,1,0:T(8,128)(2,1)S(1)}, bf16[3,64,640]{2,1,0:T(8,128)(2,1)S(1)}, u32[]{:S(2)}, u32[]{:S(2)}) collective-permute-start(bf16[3,64,640]{2,1,0:T(8,128)(2,1)S(1)} %get-tuple-element.109), channel_id=1, source_target_pairs={{0,16},{2,18},{4,20},{6,22},{8,24},{10,26},{12,28},{14,30},{16,0},... | collective-permute-start | bytes 737288 | tf_op jit(solution)/shard_map/ppermute | solution.py:564
  397.0 35.2 %collective-permute-start.57 = (bf16[3,64,640]{2,1,0:T(8,128)(2,1)S(1)}, bf16[3,64,640]{2,1,0:T(8,128)(2,1)S(1)}, u32[]{:S(2)}, u32[]{:S(2)}) collective-permute-start(bf16[3,64,640]{2,1,0:T(8,128)(2,1)S(1)} %get-tuple-element.110), channel_id=1, source_target_pairs={{0,24},{2,26},{4,28},{6,30},{8,16},{10,18},{12,20},{14,22},{16,8},... | collective-permute-start | bytes 737288 | tf_op jit(solution)/shard_map/ppermute | solution.py:564
  404.7 27.7 %collective-permute-start.47 = (bf16[3,64,768]{2,1,0:T(8,128)(2,1)S(1)}, bf16[3,64,768]{2,1,0:T(8,128)(2,1)S(1)}, u32[]{:S(2)}, u32[]{:S(2)}) collective-permute-start(bf16[3,64,768]{2,1,0:T(8,128)(2,1)S(1)} %get-tuple-element.98), channel_id=1, source_target_pairs={{0,8},{2,10},{4,12},{6,14},{8,0},{10,2},{12,4},{14,6},{16,24},{18,... | collective-permute-start | bytes 884744 | tf_op jit(solution)/shard_map/ppermute | solution.py:564
  408.0 29.0 %collective-permute-start.48 = (bf16[3,64,768]{2,1,0:T(8,128)(2,1)S(1)}, bf16[3,64,768]{2,1,0:T(8,128)(2,1)S(1)}, u32[]{:S(2)}, u32[]{:S(2)}) collective-permute-start(bf16[3,64,768]{2,1,0:T(8,128)(2,1)S(1)} %get-tuple-element.99), channel_id=1, source_target_pairs={{0,16},{2,18},{4,20},{6,22},{8,24},{10,26},{12,28},{14,30},{16,0},... | collective-permute-start | bytes 884744 | tf_op jit(solution)/shard_map/ppermute | solution.py:564
  408.1 34.7 %collective-permute-start.49 = (bf16[3,64,768]{2,1,0:T(8,128)(2,1)S(1)}, bf16[3,64,768]{2,1,0:T(8,128)(2,1)S(1)}, u32[]{:S(2)}, u32[]{:S(2)}) collective-permute-start(bf16[3,64,768]{2,1,0:T(8,128)(2,1)S(1)} %get-tuple-element.100), channel_id=1, source_target_pairs={{0,24},{2,26},{4,28},{6,30},{8,16},{10,18},{12,20},{14,22},{16,8},... | collective-permute-start | bytes 884744 | tf_op jit(solution)/shard_map/ppermute | solution.py:564
  (21 other events, 92.6 us)
